TPU v7x, 256 devices: a whole 4x4x8 slice. The times are simulated.
256 devices in a mesh: ctx: 32 (over z, x_hi, core), pipe: 8 (over y, x_lo).
Axes of the slice: x: 4 (x_hi: 2, x_lo: 2; x = x_hi * 2 + x_lo), y: 4, z: 8, core: 2. Of those that a mesh axis runs over, the one named last changes fastest.
Arguments:
- query_fwd: bfloat16 [8, 4096, 2048], P('pipe', 'ctx'), may hold values from -6 to 6
- key_fwd: bfloat16 [8, 4096, 512], P('pipe', 'ctx'), may hold values from -6 to 6
- value_fwd: bfloat16 [8, 4096, 512], P('pipe', 'ctx'), may hold values from -6 to 6
- gate_fwd: bfloat16 [8, 4096, 2048], P('pipe', 'ctx'), may hold values from -6 to 6
- types_fwd: int32 [8, 4096], P('pipe', 'ctx'), may hold values from 0 to 63
- query_bwd: bfloat16 [8, 4096, 2048], P('pipe', 'ctx'), may hold values from -6 to 6
- key_bwd: bfloat16 [8, 4096, 512], P('pipe', 'ctx'), may hold values from -6 to 6
- value_bwd: bfloat16 [8, 4096, 512], P('pipe', 'ctx'), may hold values from -6 to 6
- grad_out: bfloat16 [8, 4096, 2048], P('pipe', 'ctx'), may hold values from -6 to 6
- types_bwd: int32 [8, 4096], P('pipe', 'ctx'), may hold values from 0 to 63
- type_key: bfloat16 [8, 64, 512], P('pipe'), may hold values from -4.1875 to 4.1875
- norm_gain: float32 [8, 2048], P('pipe'), may hold values from 0.5 to 1.5
- stretch_order: int32 [8, 64], P('pipe'), may hold values from 0 to 63, as said below
Outputs:
- handed: bfloat16 [8, 4096, 2048], P('pipe', 'ctx')
- query_grad: bfloat16 [8, 4096, 2048], P('pipe', 'ctx')
- key_grad: bfloat16 [8, 4096, 512], P('pipe', 'ctx')
- value_grad: bfloat16 [8, 4096, 512], P('pipe', 'ctx')
Inputs may be any that keep to these rules, and one draw needn't show every extreme that they name: `stretch_order`: in each section's row the stored stretch slots 2 c and 2 c + 1 (those of index c of ctx) hold two stretches whose numbers add to 63, in either order; each row names every stretch once.
All inputs are finite; a program needn't handle non-finite values.
Results may differ from a plain program's by a relative error of at most 0.02.
Values may be sent and summed in bfloat16 or wider, within the bound.
A program may use at most 128 MiB of HBM per device.

v0:
```python
import math

import jax
import jax.numpy as jnp
from jax import lax
from jax.sharding import PartitionSpec as P

HEAD = 128


norm_eps = 1e-06


def from_behind(block, axis, distance):
    devices = range(lax.axis_size(axis))
    route = [((i - distance) % len(devices), i) for i in devices]
    return lax.ppermute(block, axis, route)


def silu_slope(scores):
    sigmoid_part = jax.nn.sigmoid(scores)
    return sigmoid_part * (1.0 + scores * (1.0 - sigmoid_part))


def typed_keys(key_rows, event_types, type_table):
    onehot = (
        event_types[:, None] == jnp.arange(type_table.shape[0], dtype=jnp.int32)[None, :]
    ).astype(jnp.bfloat16)
    type_rows = jnp.dot(onehot, type_table, preferred_element_type=jnp.float32)
    return (key_rows.astype(jnp.float32) + type_rows).astype(jnp.bfloat16)


def invert(stretch_perm):
    total_stretches = stretch_perm.shape[0]
    matches = stretch_perm[None, :] == jnp.arange(total_stretches, dtype=jnp.int32)[:, None]
    return jnp.sum(
        jnp.where(matches, jnp.arange(total_stretches, dtype=jnp.int32)[None, :], 0), axis=1
    )


def to_sequence(stored, inverse, stretch_rows):
    return jnp.take(stored.reshape(-1, stretch_rows, stored.shape[1]), inverse, axis=0).reshape(
        -1, stored.shape[1]
    )


def position(stretch_perm, slot_index, stretch_rows):
    leading = lax.dynamic_index_in_dim(stretch_perm, slot_index, keepdims=False)
    return leading * stretch_rows + jnp.arange(stretch_rows, dtype=jnp.int32)


def score_block(queries, query_pos, key_rows, value_rows, key_pos):
    row_count = queries.shape[0]
    kv_heads = key_rows.shape[1] // HEAD
    groups = queries.shape[1] // key_rows.shape[1]
    query_heads = queries.reshape(row_count, kv_heads, groups, HEAD)
    key_heads = key_rows.reshape(-1, kv_heads, HEAD)
    value_heads = value_rows.reshape(-1, kv_heads, HEAD)
    scores = jnp.einsum(
        "qhgd,thd->hgqt", query_heads, key_heads, preferred_element_type=jnp.float32
    ) * HEAD ** (-0.5)
    visible = key_pos[None, :] <= query_pos[:, None]
    shrink = lax.rsqrt((query_pos + 1).astype(jnp.float32))[:, None]
    weights = (jnp.where(visible, jax.nn.silu(scores), 0.0) * shrink).astype(jnp.bfloat16)
    return (query_heads, key_heads, value_heads, scores, visible, shrink, weights)


def forward_block(queries, query_pos, key_rows, value_rows, key_pos):
    query_heads, key_heads, value_heads, scores, visible, shrink, weights = score_block(
        queries, query_pos, key_rows, value_rows, key_pos
    )
    return jnp.einsum(
        "hgqt,thd->qhgd", weights, value_heads, preferred_element_type=jnp.float32
    ).reshape(queries.shape[0], -1)


def backward_block(queries, grad_rows, query_pos, key_rows, value_rows, key_pos):
    query_heads, key_heads, value_heads, scores, visible, shrink, weights = score_block(
        queries, query_pos, key_rows, value_rows, key_pos
    )
    grad_heads = grad_rows.reshape(query_heads.shape)
    weight_grad = jnp.einsum(
        "qhgd,thd->hgqt", grad_heads, value_heads, preferred_element_type=jnp.float32
    )
    score_grad = (jnp.where(visible, weight_grad * silu_slope(scores), 0.0) * shrink).astype(
        jnp.bfloat16
    )
    query_part = jnp.einsum(
        "hgqt,thd->qhgd", score_grad, key_heads, preferred_element_type=jnp.float32
    ).reshape(queries.shape[0], -1)
    key_part = jnp.einsum(
        "hgqt,qhgd->thd", score_grad, query_heads, preferred_element_type=jnp.float32
    ) * HEAD ** (-0.5)
    value_part = jnp.einsum(
        "hgqt,qhgd->thd", weights, grad_heads, preferred_element_type=jnp.float32
    )
    kv_width = key_rows.shape[1]
    return (
        query_part,
        jnp.concatenate([key_part.reshape(-1, kv_width), value_part.reshape(-1, kv_width)], axis=1),
    )


def rows_forward(queries, query_pos, seq_keys, seq_values, block_rows):
    block_count = query_pos[-1] // block_rows + 1

    def advance(step_index, running):
        offset = step_index * block_rows
        key_rows = lax.dynamic_slice_in_dim(seq_keys, offset, block_rows, 0)
        value_rows = lax.dynamic_slice_in_dim(seq_values, offset, block_rows, 0)
        key_pos = offset + jnp.arange(block_rows, dtype=jnp.int32)
        return running + forward_block(queries, query_pos, key_rows, value_rows, key_pos)

    return lax.fori_loop(0, block_count, advance, jnp.zeros(queries.shape, jnp.float32))


def rows_backward(queries, grad_rows, query_pos, seq_keys, seq_values, block_rows, buffer):
    block_count = query_pos[-1] // block_rows + 1

    def advance(step_index, carried):
        running, buffer_in = carried
        offset = step_index * block_rows
        key_rows = lax.dynamic_slice_in_dim(seq_keys, offset, block_rows, 0)
        value_rows = lax.dynamic_slice_in_dim(seq_values, offset, block_rows, 0)
        key_pos = offset + jnp.arange(block_rows, dtype=jnp.int32)
        query_part, kv_part = backward_block(
            queries, grad_rows, query_pos, key_rows, value_rows, key_pos
        )
        former = lax.dynamic_slice_in_dim(buffer_in, offset, block_rows, 0)
        return (
            running + query_part,
            lax.dynamic_update_slice_in_dim(buffer_in, former + kv_part, offset, 0),
        )

    return lax.fori_loop(0, block_count, advance, (jnp.zeros(queries.shape, jnp.float32), buffer))


def body(
    query_fwd,
    key_fwd,
    value_fwd,
    gate_fwd,
    types_fwd,
    query_bwd,
    key_bwd,
    value_bwd,
    grad_out,
    types_bwd,
    type_key,
    norm_gain,
    stretch_order,
):
    row_count = query_fwd.shape[1]
    stretch_rows = row_count // 2
    total_rows = row_count * lax.axis_size("ctx")
    block_rows = math.gcd(total_rows, 512)
    device_pos = lax.axis_index("ctx")
    stretch_perm = stretch_order[0]
    type_table = type_key[0]
    keys_f = typed_keys(key_fwd[0], types_fwd[0], type_table)
    keys_b = typed_keys(key_bwd[0], types_bwd[0], type_table)
    kv_width = keys_f.shape[1]
    queries_f = query_fwd[0]
    queries_b = query_bwd[0]
    grad_rows = grad_out[0]
    query_spans = [
        position(stretch_perm, 2 * device_pos + stretch_slot, stretch_rows)
        for stretch_slot in range(2)
    ]
    whole_keys, whole_values = (
        lax.all_gather(keys_f, "ctx", axis=0, tiled=True),
        lax.all_gather(value_fwd[0], "ctx", axis=0, tiled=True),
    )
    inverse = invert(stretch_perm)
    seq_keys = to_sequence(whole_keys, inverse, stretch_rows)
    seq_values = to_sequence(whole_values, inverse, stretch_rows)
    attended = jnp.concatenate(
        [
            rows_forward(
                queries_f[stretch_slot * stretch_rows : (stretch_slot + 1) * stretch_rows],
                query_spans[stretch_slot],
                seq_keys,
                seq_values,
                block_rows,
            )
            for stretch_slot in range(2)
        ],
        axis=0,
    )
    back_keys, back_values = (
        lax.all_gather(keys_b, "ctx", axis=0, tiled=True),
        lax.all_gather(value_bwd[0], "ctx", axis=0, tiled=True),
    )
    seq_back_keys = to_sequence(back_keys, inverse, stretch_rows)
    seq_back_values = to_sequence(back_values, inverse, stretch_rows)
    buffer = jnp.zeros((total_rows, 2 * kv_width), jnp.float32)
    query_parts = []
    for stretch_slot in range(2):
        lower = stretch_slot * stretch_rows
        query_part, buffer = rows_backward(
            queries_b[lower : lower + stretch_rows],
            grad_rows[lower : lower + stretch_rows],
            query_spans[stretch_slot],
            seq_back_keys,
            seq_back_values,
            block_rows,
            buffer,
        )
        query_parts.append(query_part)
    query_sums = jnp.concatenate(query_parts, axis=0)
    partial_value = jnp.take(
        buffer.reshape(-1, stretch_rows, 2 * kv_width), stretch_perm, axis=0
    ).reshape(total_rows, 2 * kv_width)
    mean_square = jnp.mean(attended * attended, axis=1, keepdims=True)
    gated = (
        attended
        * lax.rsqrt(mean_square + norm_eps)
        * norm_gain[0][None, :]
        * gate_fwd[0].astype(jnp.float32)
    ).astype(jnp.bfloat16)
    handed = from_behind(gated[None], "pipe", 1)
    summed = lax.psum_scatter(
        partial_value.astype(jnp.bfloat16), "ctx", scatter_dimension=0, tiled=True
    ).astype(jnp.float32)
    query_grad = (query_sums * HEAD ** (-0.5)).astype(jnp.bfloat16)
    return (
        handed,
        query_grad[None],
        summed[None, :, :kv_width].astype(jnp.bfloat16),
        summed[None, :, kv_width:].astype(jnp.bfloat16),
    )


def solution(mesh):
    placed = (
        P("pipe", "ctx", None),
        P("pipe", "ctx", None),
        P("pipe", "ctx", None),
        P("pipe", "ctx", None),
        P("pipe", "ctx"),
        P("pipe", "ctx", None),
        P("pipe", "ctx", None),
        P("pipe", "ctx", None),
        P("pipe", "ctx", None),
        P("pipe", "ctx"),
        P("pipe", None, None),
        P("pipe", None),
        P("pipe", None),
    )
    return jax.shard_map(
        body,
        mesh=mesh,
        in_specs=placed,
        out_specs=(
            P("pipe", "ctx", None),
            P("pipe", "ctx", None),
            P("pipe", "ctx", None),
            P("pipe", "ctx", None),
        ),
        check_vma=False,
    )
```

profile of v0, /device:TPU:11, one launch (start us, length us, event | category | flops | bytes accessed | tf_op | source)
XLA Modules:
  0.0 700.8 jit_solution(5016380427951543351)
XLA Ops:
  8.0 1.8 fusion.93
  9.9 1.8 fusion.94
  26.3 73.7 %all-gather.13.cloned.1.call-done = bf16[1,4096,512]{2,1,0:T(8,128)(2,1)} async-done(((bf16[1,128,512]{2,1,0:T(8,128)(2,1)}), bf16[1,4096,512]{2,1,0:T(8,128)(2,1)}) %all-gather.13.cloned.1.call-update) | async-done | bytes 4194320 | tf_op jit(solution)/shard_map/all_gather | solution.py:192
  100.1 5.0 gather_fusion.4
  105.1 81.8 %all-gather.7.cloned.1.call-done = bf16[4096,512]{1,0:T(8,128)(2,1)} async-done(((bf16[128,512]{1,0:T(8,128)(2,1)}), bf16[4096,512]{1,0:T(8,128)(2,1)}) %all-gather.7.cloned.1.call-update) | async-done | bytes 4194320 | tf_op jit(solution)/shard_map/all_gather | solution.py:171
  186.9 4.9 gather_fusion.2
  191.9 82.0 %all-gather.9.cloned.1.call-done = bf16[4096,512]{1,0:T(8,128)(2,1)} async-done(((bf16[128,512]{1,0:T(8,128)(2,1)}), bf16[4096,512]{1,0:T(8,128)(2,1)}) %all-gather.9.cloned.1.call-update) | async-done | bytes 4194320 | tf_op jit(solution)/shard_map/all_gather | solution.py:191
  273.8 5.0 gather_fusion.3
  278.8 81.2 %all-gather.11.cloned.1.call-done = bf16[1,4096,512]{2,1,0:T(8,128)(2,1)} async-done(((bf16[1,128,512]{2,1,0:T(8,128)(2,1)}), bf16[1,4096,512]{2,1,0:T(8,128)(2,1)}) %all-gather.11.cloned.1.call-update) | async-done | bytes 4194320 | tf_op jit(solution)/shard_map/all_gather | solution.py:172
  360.0 5.0 gather_fusion.1
  364.9 12.0 %broadcast_select_fusion = (bf16[64,64,512]{2,1,0:T(8,128)(2,1)}, bf16[64,64,512]{2,1,0:T(8,128)(2,1)}, bf16[64,64,512]{2,1,0:T(8,128)(2,1)}, bf16[64,64,512]{2,1,0:T(8,128)(2,1)}) fusion(bf16[64,64,512]{2,1,0:T(8,128)(2,1)} %gather_fusion.4, pred[64]{0:T(512)(128)(4,1)S(1)} %compare_and_fusion, bf16[64,64,512]{2,1,0:T(8,128)(2,1)} %gather_fusion.2, ...), kind=kLoop, calls=%fused_computation.131 | loop fusion | flops 8388608 | bytes 33554496 | tf_op jit(solution)/shard_map/jit(_take)/select_n | solution.py:42
  377.0 6.4 copy.115
  383.4 6.4 copy.116
  389.8 7.9 %broadcast_in_dim.93 = f32[4096,1024]{0,1:T(8,128)} broadcast(f32[]{:T(128)} %constant.136.clone.1), dimensions={} | broadcast | bytes 16777220 | tf_op jit(solution)/shard_map/broadcast_in_dim | solution.py:196
  397.7 34.8 %while.54 = (s32[]{:T(128)}, f32[64,2048]{1,0:T(8,128)S(1)}, f32[4096,1024]{0,1:T(8,128)}, s32[]{:T(128)}, bf16[4096,512]{0,1:T(8,128)(2,1)}, /*index=5*/bf16[40...) while((s32[]{:T(128)}, f32[64,2048]{1,0:T(8,128)S(1)}, ...), condition=%wide.wide.region_7.9_spmd.clone, body=%wide.wide.region_6.8_spmd.clone.sunk | while | flops 683049728 | bytes 35231216 | solution.py:135
  399.6 2.3 fusion.214
  403.0 2.5 fusion.215
  405.9 3.4 fusion.217
  411.1 2.3 fusion.214
  414.6 2.5 fusion.215
  417.5 3.4 fusion.217
  422.7 2.3 fusion.214
  426.1 2.5 fusion.215
  429.0 3.5 fusion.217
  433.3 73.1 %while.55 = (s32[]{:T(128)}, f32[64,2048]{1,0:T(8,128)}, f32[4096,1024]{0,1:T(8,128)}, s32[]{:T(128)}, bf16[4096,512]{0,1:T(8,128)(2,1)}, /*index=5*/bf16[4096,5...) while((s32[]{:T(128)}, f32[64,2048]{1,0:T(8,128)}, ...), condition=%wide.wide.region_9.11_spmd.clone, body=%wide.wide.region_8.10_spmd.clone.sunk | while | flops 683049728 | bytes 35231216 | solution.py:135
  437.3 1.9 add.599
  439.2 2.5 fusion.230
  442.1 3.4 fusion.232
  449.5 1.9 add.599
  451.4 2.5 fusion.230
  454.3 3.4 fusion.232
  461.7 1.9 add.599
  463.6 2.5 fusion.230
  466.5 3.5 fusion.232
  473.9 1.9 add.599
  475.8 2.5 fusion.230
  478.7 3.4 fusion.232
  486.1 1.9 add.599
  488.0 2.5 fusion.230
  490.9 3.4 fusion.232
  498.3 1.9 add.599
  500.2 2.5 fusion.230
  503.1 3.4 fusion.232
  506.5 13.9 %copy.119 = bf16[4096,1024]{1,0:T(8,128)(2,1)} copy(f32[4096,1024]{0,1:T(8,128)} %get-tuple-element.184) | data formatting | bytes 25165824 | tf_op jit(solution)/shard_map/while | solution.py:135
  520.3 9.1 %gather_fusion = bf16[64,64,1024]{2,1,0:T(8,128)(2,1)} fusion(bf16[64,64,1024]{2,1,0:T(8,128)(2,1)} %bitcast.387, s32[1024]{0:T(1024)} %pad_clamp_fusion), kind=kCustom, calls=%fused_computation.4 | custom fusion | bytes 16777472 | tf_op jit(solution)/shard_map/jit(_take)/gather | solution.py:211
  529.4 7.6 %fusion.92 = bf16[4096,1024]{1,0:T(8,128)(2,1)} fusion(bf16[64,64,1024]{2,1,0:T(8,128)(2,1)} %gather_fusion, pred[4096]{0:T(1024)(128)(4,1)S(1)} %copy-done.14), kind=kLoop, calls=%fused_computation.130 | loop fusion | flops 4194304 | bytes 16781312 | tf_op jit(solution)/shard_map/convert_element_type | solution.py:223
  539.9 6.4 copy.111
  546.3 6.5 copy.112
  552.8 25.5 %while.53 = (s32[]{:T(128)}, f32[64,2048]{1,0:T(8,128)S(1)}, s32[]{:T(128)}, bf16[4096,512]{0,1:T(8,128)(2,1)}, bf16[4096,512]{0,1:T(8,128)(2,1)}, /*index=5*/bf...) while((s32[]{:T(128)}, f32[64,2048]{1,0:T(8,128)S(1)}, ...), condition=%wide.wide.region_4.6_spmd.clone, body=%wide.wide.region_3.5_spmd.clone.sunk | while | flops 272794368 | bytes 7673019 | solution.py:114
  554.4 2.1 fusion.202
  558.6 2.1 fusion.202
  562.8 2.1 fusion.202
  567.1 2.1 fusion.202
  571.4 2.1 fusion.202
  575.6 2.0 fusion.202
  578.5 15.2 %while.52 = (s32[]{:T(128)}, f32[64,2048]{1,0:T(8,128)S(1)}, s32[]{:T(128)}, bf16[4096,512]{0,1:T(8,128)(2,1)}, bf16[4096,512]{0,1:T(8,128)(2,1)}, /*index=5*/bf...) while((s32[]{:T(128)}, f32[64,2048]{1,0:T(8,128)S(1)}, ...), condition=%wide.wide.region_2.4_spmd.clone, body=%wide.wide.region_1.3_spmd.clone.sunk | while | flops 272794368 | bytes 7673019 | solution.py:114
  579.9 1.9 fusion.198
  581.8 1.4 copy.205
  585.0 1.9 fusion.198
  590.0 1.9 fusion.198
  595.2 3.0 collective-permute-start
  599.1 13.8 %collective-permute-done = bf16[1,128,2048]{2,1,0:T(8,128)(2,1)S(1)} collective-permute-done((bf16[1,128,2048]{2,1,0:T(8,128)(2,1)S(1)}, bf16[1,128,2048]{2,1,0:T(8,128)(2,1)S(1)}, u32[]{:S(2)}, u32[]{:S(2)}) %collective-permute-start) | collective-permute-done | bytes 524320 | tf_op jit(solution)/shard_map/ppermute | solution.py:17
  612.9 78.8 %reduce-scatter.2.cloned.1.call-done = bf16[128,1024]{1,0:T(8,128)(2,1)} async-done(((bf16[4096,1024]{1,0:T(8,128)(2,1)}), bf16[128,1024]{1,0:T(8,128)(2,1)}) %reduce-scatter.2.cloned.1.call-update) | async-done | bytes 262160 | tf_op jit(solution)/shard_map/reduce_scatter | solution.py:222
  691.7 1.7 slice_bitcast_fusion.6
  (259 shorter events, 71.8 us)
Async XLA Ops:
  7.2 0.8 copy-start
  7.2 92.9 %all-gather.13.cloned.1.call-start = ((), (), s32[]{:S(2)}) async-start(), calls=%async_computation.5 | async-start | bytes 4325376 | tf_op jit(solution)/shard_map/all_gather | solution.py:192
  7.9 179.0 %all-gather.7.cloned.1.call-start = ((), (), s32[]{:S(2)}) async-start(), calls=%async_computation.1 | async-start | bytes 4325376 | tf_op jit(solution)/shard_map/all_gather | solution.py:171
  9.8 264.0 %all-gather.9.cloned.1.call-start = ((), (), s32[]{:S(2)}) async-start(), calls=%async_computation.2 | async-start | bytes 4325376 | tf_op jit(solution)/shard_map/all_gather | solution.py:191
  11.7 348.3 %all-gather.11.cloned.1.call-start = ((), (), s32[]{:S(2)}) async-start(), calls=%async_computation.4 | async-start | bytes 4325376 | tf_op jit(solution)/shard_map/all_gather | solution.py:172
  12.3 679.4 %reduce-scatter.2.cloned.1.call-start = ((), (), s32[]{:S(2)}) async-start(), calls=%async_computation.3 | async-start | bytes 8650752 | tf_op jit(solution)/shard_map/reduce_scatter | solution.py:222
  21.4 3.4 copy-start.16
  22.7 82.4 %copy-start.7 = (bf16[64,2048]{1,0:T(8,128)(2,1)}, bf16[64,2048]{1,0:T(8,128)(2,1)S(1)}, u32[]{:S(2)}) copy-start(bf16[64,2048]{1,0:T(8,128)(2,1)S(1)} %get-tuple-element.931) | copy-start | bytes 786436
  22.7 82.4 %copy-start.8 = (bf16[64,2048]{1,0:T(8,128)(2,1)}, bf16[64,2048]{1,0:T(8,128)(2,1)S(1)}, u32[]{:S(2)}) copy-start(bf16[64,2048]{1,0:T(8,128)(2,1)S(1)} %get-tuple-element.930) | copy-start | bytes 786436
  22.7 82.4 %copy-start.9 = (bf16[64,2048]{1,0:T(8,128)(2,1)}, bf16[64,2048]{1,0:T(8,128)(2,1)S(1)}, u32[]{:S(2)}) copy-start(bf16[64,2048]{1,0:T(8,128)(2,1)S(1)} %get-tuple-element.886) | copy-start | bytes 786436
  22.7 82.4 %copy-start.10 = (bf16[64,2048]{1,0:T(8,128)(2,1)}, bf16[64,2048]{1,0:T(8,128)(2,1)S(1)}, u32[]{:S(2)}) copy-start(bf16[64,2048]{1,0:T(8,128)(2,1)S(1)} %get-tuple-element.885) | copy-start | bytes 786436
  397.7 35.7 %copy-start.12 = (bf16[64,4,4,128]{3,2,1,0:T(4,128)(2,1)S(1)}, bf16[64,4,4,128]{3,2,1,0:T(4,128)(2,1)}, u32[]{:S(2)}) copy-start(bf16[64,4,4,128]{3,2,1,0:T(4,128)(2,1)} %reshape.435) | copy-start | bytes 786436
  399.4 2.4 copy-start.2
  411.0 2.4 copy-start.2
  422.6 2.4 copy-start.2
  435.0 1.3 copy-start.3
  447.2 1.3 copy-start.3
  459.4 1.3 copy-start.3
  471.6 1.3 copy-start.3
  483.8 1.3 copy-start.3
  496.0 1.3 copy-start.3
  520.3 9.1 %copy-start.14 = (pred[4096]{0:T(1024)(128)(4,1)S(1)}, pred[4096]{0:T(1024)(128)(4,1)}, u32[]{:S(2)}) copy-start(pred[4096]{0:T(1024)(128)(4,1)} %broadcast_in_dim.95) | copy-start | bytes 12292
  537.1 1.0 copy-start.11
  538.1 8.1 %copy-start.5 = (bf16[64,2048]{1,0:T(8,128)(2,1)}, bf16[64,2048]{1,0:T(8,128)(2,1)S(1)}, u32[]{:S(2)}) copy-start(bf16[64,2048]{1,0:T(8,128)(2,1)S(1)} %get-tuple-element.848) | copy-start | bytes 786436
  538.2 8.1 %copy-start.6 = (bf16[64,2048]{1,0:T(8,128)(2,1)}, bf16[64,2048]{1,0:T(8,128)(2,1)S(1)}, u32[]{:S(2)}) copy-start(bf16[64,2048]{1,0:T(8,128)(2,1)S(1)} %get-tuple-element.812) | copy-start | bytes 786436
  552.8 25.6 %copy-start.13 = (bf16[64,4,4,128]{3,2,1,0:T(4,128)(2,1)S(1)}, bf16[64,4,4,128]{3,2,1,0:T(4,128)(2,1)}, u32[]{:S(2)}) copy-start(bf16[64,4,4,128]{3,2,1,0:T(4,128)(2,1)} %reshape.423) | copy-start | bytes 786436
  578.4 15.4 %copy-start.15 = (f32[1,2048]{1,0:T(1,128)S(1)}, f32[1,2048]{1,0:T(1,128)}, u32[]{:S(2)}) copy-start(f32[1,2048]{1,0:T(1,128)} %param.34) | copy-start | bytes 24580
  593.7 4.5 copy-start.4
  593.9 100.3 %copy-start.1 = (bf16[1,64,512]{2,1,0:T(8,128)(2,1)S(1)}, bf16[1,64,512]{2,1,0:T(8,128)(2,1)}, u32[]{:S(2)}) copy-start(bf16[1,64,512]{2,1,0:T(8,128)(2,1)} %param.33) | copy-start | bytes 196612
  595.2 17.7 %collective-permute-start = (bf16[1,128,2048]{2,1,0:T(8,128)(2,1)S(1)}, bf16[1,128,2048]{2,1,0:T(8,128)(2,1)S(1)}, u32[]{:S(2)}, u32[]{:S(2)}) collective-permute-start(bf16[1,128,2048]{2,1,0:T(8,128)(2,1)S(1)} %fusion.97), channel_id=1, source_target_pairs={{7,0},{0,1},{1,2},{2,3},{3,4},{4,5},{5,6},{6,7},{15,8},{8,9},{9,10... | collective-permute-start | bytes 1572872 | tf_op jit(solution)/shard_map/ppermute | solution.py:17
Sparse Core Ops, SparseCore 0:
  10.8 89.2 all-gather.12
  103.4 83.4 all-gather.6
  190.3 83.4 all-gather.8
  276.5 83.4 all-gather.10
  537.2 154.4 reduce-scatter.1
where the time goes:
time: 709 us; the launch traced here: 701 us
  waiting for transfers between devices  413 us (58%)
  local copies, waits for them, and re-layouts  126 us (18%)
  matrix products  68.8 us (10%)
  other arithmetic  68.2 us (10%)
  between operations  20.5 us (3%)
    all_gather x1, waiting for transfers between devices, body(): lax.all_gather(keys_b, 'ctx', axis=0, tiled=True)  82 us
    all_gather x1, waiting for transfers between devices, body(): lax.all_gather(keys_f, 'ctx', axis=0, tiled=True)  81.8 us
    all_gather x1, waiting for transfers between devices, body(): lax.all_gather(value_fwd[0], 'ctx', axis=0, tiled=True)  81.2 us
    reduce_scatter x1, waiting for transfers between devices, body(): lax.psum_scatter(partial_value.astype(jnp.bfloat16), 'ctx', scatter_dimen...  78.8 us
    all_gather x1, waiting for transfers between devices, body(): lax.all_gather(value_bwd[0], 'ctx', axis=0, tiled=True)  73.7 us
    dynamic_update_slice x9, other arithmetic, advance(): lax.dynamic_update_slice_in_dim(buffer_in, former + kv_part, offset, 0)  30.7 us
    unnamed x35, local copies, waits for them, and re-layouts  27.6 us
    dot_general x9, matrix products, backward_block(): jnp.einsum('hgqt,qhgd->thd', weights, grad_heads, preferred_element_type=...  22.8 us
  transfers between devices with their start and end apart: 6, of which 6 were waited for; matrix products, arithmetic and copies ran while one was open for 12% of the time, Pallas kernels for 0%

commit v1 on v0

v1 whole, which is shorter than its diff:
```python
import functools

import jax
import jax.numpy as jnp
from jax import lax
from jax.experimental import pallas as pl
from jax.experimental.pallas import tpu as pltpu
from jax.sharding import PartitionSpec as P

HEAD = 128
ROWS = 128
HALF = 64
GROUP = 4
RING = 8
CTX = GROUP * RING
TOKENS = CTX * ROWS
BLOCK = 256
EPS = 1e-06
SCALE = HEAD**-0.5
BF = jnp.bfloat16
F32 = jnp.float32
MESH = pl.DeviceIdType.MESH
VMEM = pl.BlockSpec(memory_space=pltpu.VMEM)
ANY = pl.BlockSpec(memory_space=pl.ANY)


def place():
    me = lax.axis_index("ctx")
    z = me // GROUP
    m = me % GROUP
    x, c = m // 2, m % 2
    peers = (2 * x + (1 - c), 2 * (1 - x) + c, 2 * (1 - x) + (1 - c))
    return z, m, peers


def ctx_of(z, m):
    return {"ctx": ((z + RING) % RING) * GROUP + m}


def remote(src, dst, send, recv, target):
    return pltpu.make_async_remote_copy(
        src_ref=src,
        dst_ref=dst,
        send_sem=send,
        recv_sem=recv,
        device_id=target,
        device_id_type=MESH,
    )


def greet(targets):
    barrier = pltpu.get_barrier_semaphore()
    for target in targets:
        pl.semaphore_signal(barrier, inc=1, device_id=target, device_id_type=MESH)
    return lambda: pl.semaphore_wait(barrier, len(targets))


def gather_kernel(
    types_f, types_b, table, qf, kf, vf, qb, kb, vb, go,
    out_q, out_f, out_b,
    stage_q, stage_kv, local_sem, a_send, a_recv, r_send, r_recv,
):
    z, m, peers = place()
    greeted = greet(
        [ctx_of(z, p) for p in peers] + [ctx_of(z + 1, m), ctx_of(z - 1, m)]
    )
    outs = (out_f, out_b)
    for t, (types, keys, values) in enumerate(((types_f, kf, vf), (types_b, kb, vb))):
        kinds = lax.broadcasted_iota(jnp.int32, (table.shape[0], ROWS), 0)
        onehot = jnp.where(kinds == types[...], 1.0, 0.0).astype(BF)
        rows = lax.dot_general(
            onehot, table[...], (((0,), (0,)), ((), ())), preferred_element_type=F32
        )
        typed = (keys[...].astype(F32) + rows).astype(BF)
        for h in range(GROUP):
            stage_kv[t, h, 0] = typed[:, h * HEAD : (h + 1) * HEAD]
            stage_kv[t, h, 1] = values[:, h * HEAD : (h + 1) * HEAD]
    greeted()
    started = []
    arrivals_kv = []
    for t in range(2):
        arriving = []
        for d, p in enumerate(peers):
            copy = remote(
                stage_kv.at[t, p], outs[t].at[z * GROUP + m],
                a_send.at[d, t], a_recv.at[d, t], ctx_of(z, p),
            )
            copy.start()
            arriving.append(copy)
            started.append(copy)
        arrivals_kv.append(arriving)
    own = []
    for t in range(2):
        copy = pltpu.make_async_copy(
            stage_kv.at[t, m], outs[t].at[z * GROUP + m], local_sem.at[t]
        )
        copy.start()
        own.append(copy)
    arrivals_q = []
    for t, source in enumerate((qf, qb, go)):
        for h in range(GROUP):
            for g in range(4):
                col = (h * 4 + g) * HEAD
                stage_q[t, h, g] = source[:, col : col + HEAD]
        for d, p in enumerate(peers):
            copy = remote(
                stage_q.at[t, p], out_q.at[t, m],
                a_send.at[d, 2 + t], a_recv.at[d, 2 + t], ctx_of(z, p),
            )
            copy.start()
            arrivals_q.append(copy)
            started.append(copy)
        copy = pltpu.make_async_copy(
            stage_q.at[t, m], out_q.at[t, m], local_sem.at[2 + t]
        )
        copy.start()
        own.append(copy)

    def hop(t, step, way):
        chunk = ((z - way * (step - 1) + RING) % RING) * GROUP
        first, count = (0, GROUP) if step < RING // 2 else ((1 - way), 2)
        part = outs[t].at[pl.ds(chunk + first, count)]
        lane = 0 if way == 1 else 1
        copy = remote(
            part, part, r_send.at[t, lane, step - 1], r_recv.at[t, lane, step - 1],
            ctx_of(z + way, m),
        )
        copy.start()
        started.append(copy)
        return copy

    moving = {}
    for t in range(2):
        own[t].wait()
        for copy in arrivals_kv[t]:
            copy.wait_recv()
        for way in (1, -1):
            moving[t, way] = hop(t, 1, way)
    for step in range(2, RING // 2 + 1):
        for t in range(2):
            for way in (1, -1):
                moving[t, way].wait_recv()
                moving[t, way] = hop(t, step, way)
    for t in range(2):
        for way in (1, -1):
            moving[t, way].wait_recv()
    for copy in arrivals_q:
        copy.wait_recv()
    for copy in started:
        copy.wait_send()
    for copy in own[2:]:
        copy.wait()


def dot_nt(a, b):
    return lax.dot_general(a, b, (((1,), (1,)), ((), ())), preferred_element_type=F32)


def dot_nn(a, b):
    return jnp.dot(a, b, preferred_element_type=F32)


def attention_kernel(
    order, q_all, kv_f, kv_b, att, dq, dkv,
    ks, vs, kt, dk, dv, acc, acc_t,
):
    z = lax.axis_index("ctx") // GROUP

    def unsort(kv):
        def fill(j, _):
            for half in range(2):
                at = pl.ds(pl.multiple_of(order[2 * j + half] * HALF, HALF), HALF)
                ks[at, :] = kv[j, 0, half * HALF : (half + 1) * HALF]
                vs[at, :] = kv[j, 1, half * HALF : (half + 1) * HALF]
            return 0

        lax.fori_loop(0, CTX, fill, 0)

    def shrink_rows(stretch):
        row = lax.broadcasted_iota(jnp.int32, (4 * HALF, HEAD), 0) % HALF
        return lax.rsqrt((stretch * HALF + row + 1).astype(F32))

    unsort(kv_f)

    def forward(i, _):
        s, half = i // 2, i % 2
        stretch = order[2 * GROUP * z + i]
        rows = pl.ds(pl.multiple_of(half * HALF, HALF), HALF)
        q = q_all[0, s, :, rows, :].reshape(4 * HALF, HEAD)
        acc[...] = jnp.zeros_like(acc)

        def step(b, masked):
            at = pl.ds(pl.multiple_of(b * BLOCK, BLOCK), BLOCK)
            u = dot_nt(q, ks[at, :]) * (0.5 * SCALE)
            w = u + u * jnp.tanh(u)
            if masked:
                row = lax.broadcasted_iota(jnp.int32, w.shape, 0) % HALF
                col = lax.broadcasted_iota(jnp.int32, w.shape, 1)
                w = jnp.where(col + b * BLOCK <= row + stretch * HALF, w, 0.0)
            acc[...] += dot_nn(w.astype(BF), vs[at, :])

        full = stretch * HALF // BLOCK

        def loop(b, _):
            step(b, False)
            return 0

        lax.fori_loop(0, full, loop, 0)
        step(full, True)
        att[s, :, rows, :] = (
            (acc[...] * shrink_rows(stretch)).astype(BF).reshape(4, HALF, HEAD)
        )
        return 0

    lax.fori_loop(0, 2 * GROUP, forward, 0)

    unsort(kv_b)

    def turn(b, _):
        at = pl.ds(pl.multiple_of(b * BLOCK, BLOCK), BLOCK)
        kt[:, at] = ks[at, :].T
        dk[at, :] = jnp.zeros((BLOCK, HEAD), F32)
        dv[at, :] = jnp.zeros((BLOCK, HEAD), F32)
        return 0

    lax.fori_loop(0, TOKENS // BLOCK, turn, 0)

    def backward(i, _):
        s, half = i // 2, i % 2
        stretch = order[2 * GROUP * z + i]
        rows = pl.ds(pl.multiple_of(half * HALF, HALF), HALF)
        q = q_all[1, s, :, rows, :].reshape(4 * HALF, HEAD)
        g = q_all[2, s, :, rows, :].reshape(4 * HALF, HEAD)
        g = (g.astype(F32) * shrink_rows(stretch)).astype(BF)
        acc_t[...] = jnp.zeros_like(acc_t)

        def step(b, masked):
            at = pl.ds(pl.multiple_of(b * BLOCK, BLOCK), BLOCK)
            u = dot_nt(ks[at, :], q) * (0.5 * SCALE)
            grad = dot_nt(vs[at, :], g)
            t = jnp.tanh(u)
            ut = u * t
            w = u + ut
            slope = (0.5 + 0.5 * t) * (1.0 + (u - ut)) * grad
            if masked:
                row = lax.broadcasted_iota(jnp.int32, w.shape, 0)
                col = lax.broadcasted_iota(jnp.int32, w.shape, 1) % HALF
                seen = row + b * BLOCK <= col + stretch * HALF
                w = jnp.where(seen, w, 0.0)
                slope = jnp.where(seen, slope, 0.0)
            w = w.astype(BF)
            slope = slope.astype(BF)
            dv[at, :] += dot_nn(w, g)
            dk[at, :] += dot_nn(slope, q)
            acc_t[...] += dot_nn(kt[:, at], slope)

        full = stretch * HALF // BLOCK

        def loop(b, _):
            step(b, False)
            return 0

        lax.fori_loop(0, full, loop, 0)
        step(full, True)
        dq[s, :, rows, :] = (
            (acc_t[...] * SCALE).T.astype(BF).reshape(4, HALF, HEAD)
        )
        return 0

    lax.fori_loop(0, 2 * GROUP, backward, 0)

    def store(j, _):
        for half in range(2):
            at = pl.ds(pl.multiple_of(order[2 * j + half] * HALF, HALF), HALF)
            dkv[j, 0, half * HALF : (half + 1) * HALF] = (dk[at, :] * SCALE).astype(BF)
            dkv[j, 1, half * HALF : (half + 1) * HALF] = dv[at, :].astype(BF)
        return 0

    lax.fori_loop(0, CTX, store, 0)


def scatter_kernel(
    dkv, att, dq, gate, gain,
    handed, query_grad, key_grad, value_grad,
    sums, landed, total, att_in, dq_in, dkv_in, gated,
    r_send, r_recv, a_send, a_recv, h_send, h_recv,
):
    z, m, peers = place()
    sections = lax.axis_size("pipe")
    after = {"pipe": (lax.axis_index("pipe") + 1) % sections}
    before = {"pipe": (lax.axis_index("pipe") + sections - 1) % sections}
    greet(
        [ctx_of(z, p) for p in peers]
        + [ctx_of(z + 1, m), ctx_of(z - 1, m), after, before]
    )()
    started = []

    def exchange(t, source, target):
        copies = []
        for d, p in enumerate(peers):
            copy = remote(
                source.at[p], target.at[m], a_send.at[d, t], a_recv.at[d, t], ctx_of(z, p)
            )
            copy.start()
            copies.append(copy)
            started.append(copy)
        return copies

    def hop(step, way, part):
        chunk = ((z + way * (RING // 2 - step) + RING) % RING) * GROUP
        lane = 0 if way == 1 else 1
        mine = pl.ds(chunk + 2 * part, 2)
        if step == 0 or (step == 1 and part != lane):
            source = dkv.at[mine]
        else:
            arrived = landed[lane, step - 1, part].astype(F32)
            sums[lane, step - 1, part] = (dkv[mine].astype(F32) + arrived).astype(BF)
            source = sums.at[lane, step - 1, part]
        copy = remote(
            source, landed.at[lane, step, part],
            r_send.at[lane, step, part], r_recv.at[lane, step, part], ctx_of(z + way, m),
        )
        copy.start()
        started.append(copy)
        return copy

    att_copies = exchange(0, att, att_in)
    moving = {}
    for way, part in ((1, 0), (-1, 1)):
        moving[way, part] = hop(0, way, part)
    for way, part in ((1, 1), (-1, 0)):
        moving[way, part] = hop(1, way, part)
    for way, part in ((1, 0), (-1, 1)):
        moving[way, part].wait_recv()
        moving[way, part] = hop(1, way, part)
    dq_copies = exchange(1, dq, dq_in)

    for copy in att_copies:
        copy.wait_recv()
    att_in[m] = att[m]
    squares = jnp.zeros((ROWS, HEAD), F32)
    for h in range(GROUP):
        for g in range(4):
            part = att_in[h, g].astype(F32)
            squares += part * part
    mean = jnp.sum(squares, axis=1, keepdims=True) * (1.0 / (16 * HEAD))
    factor = lax.rsqrt(mean + EPS)
    for h in range(GROUP):
        for g in range(4):
            cols = slice((h * 4 + g) * HEAD, (h * 4 + g + 1) * HEAD)
            gated[:, cols] = (
                att_in[h, g].astype(F32) * factor * gain[:, cols] * gate[:, cols].astype(F32)
            ).astype(BF)
    hand = remote(gated, handed, h_send, h_recv, after)
    hand.start()

    for step in (2, 3):
        for part in range(2):
            for way in (1, -1):
                moving[way, part].wait_recv()
                moving[way, part] = hop(step, way, part)

    for copy in dq_copies:
        copy.wait_recv()
    dq_in[m] = dq[m]
    for h in range(GROUP):
        for g in range(4):
            cols = slice((h * 4 + g) * HEAD, (h * 4 + g + 1) * HEAD)
            query_grad[:, cols] = dq_in[h, g]

    for part in range(2):
        for way in (1, -1):
            moving[way, part].wait_recv()
        mine = pl.ds(z * GROUP + 2 * part, 2)
        total[2 * part : 2 * part + 2] = (
            dkv[mine].astype(F32)
            + landed[0, RING // 2 - 1, part].astype(F32)
            + landed[1, RING // 2 - 1, part].astype(F32)
        ).astype(BF)
    kv_copies = exchange(2, total, dkv_in)
    dkv_in[m] = total[m]
    for copy in kv_copies:
        copy.wait_recv()
    for h in range(GROUP):
        cols = slice(h * HEAD, (h + 1) * HEAD)
        key_grad[:, cols] = dkv_in[h, 0]
        value_grad[:, cols] = dkv_in[h, 1]
    for copy in started:
        copy.wait_send()
    hand.wait()


def body(
    query_fwd, key_fwd, value_fwd, gate_fwd, types_fwd,
    query_bwd, key_bwd, value_bwd, grad_out, types_bwd,
    type_key, norm_gain, stretch_order,
):
    dma, tile = pltpu.SemaphoreType.DMA, (HEAD, HEAD)
    params = functools.partial(
        pltpu.CompilerParams, vmem_limit_bytes=56 * 1024 * 1024
    )
    q_all, kv_f, kv_b = pl.pallas_call(
        gather_kernel,
        out_shape=(
            jax.ShapeDtypeStruct((3, GROUP, 4, *tile), BF),
            jax.ShapeDtypeStruct((CTX, 2, *tile), BF),
            jax.ShapeDtypeStruct((CTX, 2, *tile), BF),
        ),
        in_specs=[VMEM] * 10,
        out_specs=(ANY, ANY, ANY),
        scratch_shapes=[
            pltpu.VMEM((3, GROUP, 4, *tile), BF),
            pltpu.VMEM((2, GROUP, 2, *tile), BF),
            dma((5,)),
            dma((3, 5)),
            dma((3, 5)),
            dma((2, 2, RING // 2)),
            dma((2, 2, RING // 2)),
        ],
        compiler_params=params(collective_id=0, has_side_effects=True),
        name="gather",
    )(
        types_fwd, types_bwd, type_key[0], query_fwd[0], key_fwd[0], value_fwd[0],
        query_bwd[0], key_bwd[0], value_bwd[0], grad_out[0],
    )
    att, dq, dkv = pl.pallas_call(
        attention_kernel,
        out_shape=(
            jax.ShapeDtypeStruct((GROUP, 4, *tile), BF),
            jax.ShapeDtypeStruct((GROUP, 4, *tile), BF),
            jax.ShapeDtypeStruct((CTX, 2, *tile), BF),
        ),
        in_specs=[pl.BlockSpec(memory_space=pltpu.SMEM), VMEM, VMEM, VMEM],
        out_specs=(VMEM, VMEM, VMEM),
        scratch_shapes=[
            pltpu.VMEM((TOKENS, HEAD), BF),
            pltpu.VMEM((TOKENS, HEAD), BF),
            pltpu.VMEM((HEAD, TOKENS), BF),
            pltpu.VMEM((TOKENS, HEAD), F32),
            pltpu.VMEM((TOKENS, HEAD), F32),
            pltpu.VMEM((4 * HALF, HEAD), F32),
            pltpu.VMEM((HEAD, 4 * HALF), F32),
        ],
        compiler_params=params(),
        name="attention",
    )(stretch_order[0], q_all, kv_f, kv_b)
    wide, narrow = (ROWS, 16 * HEAD), (ROWS, GROUP * HEAD)
    handed, query_grad, key_grad, value_grad = pl.pallas_call(
        scatter_kernel,
        out_shape=(
            jax.ShapeDtypeStruct(wide, BF),
            jax.ShapeDtypeStruct(wide, BF),
            jax.ShapeDtypeStruct(narrow, BF),
            jax.ShapeDtypeStruct(narrow, BF),
        ),
        in_specs=[VMEM] * 5,
        out_specs=(ANY, VMEM, VMEM, VMEM),
        scratch_shapes=[
            pltpu.VMEM((2, RING // 2 - 1, 2, 2, 2, *tile), BF),
            pltpu.VMEM((2, RING // 2, 2, 2, 2, *tile), BF),
            pltpu.VMEM((GROUP, 2, *tile), BF),
            pltpu.VMEM((GROUP, 4, *tile), BF),
            pltpu.VMEM((GROUP, 4, *tile), BF),
            pltpu.VMEM((GROUP, 2, *tile), BF),
            pltpu.VMEM(wide, BF),
            dma((2, RING // 2, 2)),
            dma((2, RING // 2, 2)),
            dma((3, 3)),
            dma((3, 3)),
            dma,
            dma,
        ],
        compiler_params=params(collective_id=1, has_side_effects=True),
        name="scatter",
    )(dkv, att, dq, gate_fwd[0], norm_gain)
    return handed[None], query_grad[None], key_grad[None], value_grad[None]


def solution(mesh):
    rows = P("pipe", "ctx", None)
    section = P("pipe", None)
    types = P("pipe", "ctx")
    return jax.shard_map(
        body,
        mesh=mesh,
        in_specs=(
            rows, rows, rows, rows, types, rows, rows, rows, rows, types,
            P("pipe", None, None), section, section,
        ),
        out_specs=(rows, rows, rows, rows),
        check_vma=False,
    )
```

time: 709 us -> 163 us (0.23)
  the two profiles are of different devices: /device:TPU:11 before, /device:TPU:1 now
where the time goes in v1:
time: 163 us
  Pallas kernels  157 us (96%)
  local copies, waits for them, and re-layouts  5.12 us (3%)
    pallas_call x1, Pallas kernels, body(): pl.pallas_call(attention_kernel, out_shape=(jax.ShapeDtypeStruct((GROUP,...  63.5 us
    pallas_call x1, Pallas kernels, body(): pl.pallas_call(gather_kernel, out_shape=(jax.ShapeDtypeStruct((3, GROUP,...  57.3 us
    pallas_call x1, Pallas kernels, body(): pl.pallas_call(scatter_kernel, out_shape=(jax.ShapeDtypeStruct(wide, BF),...  35.9 us
    unnamed x8, local copies, waits for them, and re-layouts  5.12 us

profile of v1, /device:TPU:1, one launch (start us, length us, event | category | flops | bytes accessed | tf_op | source)
XLA Modules:
  0.0 162.5 jit_solution(5094429751473430101)
XLA Ops:
  0.6 57.3 %gather.1 = (bf16[3,4,4,128,128]{4,3,2,1,0:T(8,128)(2,1)}, bf16[32,2,128,128]{3,2,1,0:T(8,128)(2,1)}, bf16[32,2,128,128]{3,2,1,0:T(8,128)(2,1)}) custom-call(s32[1,128]{1,0:T(1,128)} %types_f.1, s32[1,128]{1,0:T(1,128)} %types_b.1, bf16[64,512]{1,0:T(8,128)(2,1)} %bitcast.26, bf16[128,2048]{1,0:T(8,128)(2,1)} %bitcast.17, bf16[128,512]{1,0:T(8,128)(2,1)} %bitcast.22, ...), custom_call_target="tpu_custom_call" | custom-call | tf_op jit(solution)/shard_map/gather/pallas_call | solution.py:402
  58.0 63.5 %attention.1 = (bf16[4,4,128,128]{3,2,1,0:T(8,128)(2,1)}, bf16[4,4,128,128]{3,2,1,0:T(8,128)(2,1)}, bf16[32,2,128,128]{3,2,1,0:T(8,128)(2,1)}) custom-call(s32[64]{0:T(128)} %bitcast.27, bf16[3,4,4,128,128]{4,3,2,1,0:T(8,128)(2,1)} %get-tuple-element.14.q_all, bf16[32,2,128,128]{3,2,1,0:T(8,128)(2,1)} %get-tuple-element.15.kv_f, ...), custom_call_target="tpu_custom_call" | custom-call | tf_op jit(solution)/shard_map/attention/pallas_call | solution.py:426
  121.5 35.9 %scatter.1 = (bf16[128,2048]{1,0:T(8,128)(2,1)}, bf16[128,2048]{1,0:T(8,128)(2,1)}, bf16[128,512]{1,0:T(8,128)(2,1)}, bf16[128,512]{1,0:T(8,128)(2,1)}) custom-call(bf16[32,2,128,128]{3,2,1,0:T(8,128)(2,1)} %get-tuple-element.17.dkv, bf16[4,4,128,128]{3,2,1,0:T(8,128)(2,1)} %get-tuple-element.18.att, bf16[4,4,128,128]{3,2,1,0:T(8,128)(2,1)} %get-tuple-element.19.dq, ...), custom_call_target="tpu_custom_call" | custom-call | tf_op jit(solution)/shard_map/scatter/pallas_call | solution.py:448
  157.4 0.0 copy-start.1
  157.4 0.0 copy-start
  157.4 1.9 %copy.21 = bf16[1,128,2048]{2,1,0:T(8,128)(2,1)} copy(bf16[1,128,2048]{2,1,0:T(8,128)(2,1)} %bitcast.16) | data formatting | bytes 1048576
  159.3 1.9 %copy.22 = bf16[1,128,2048]{2,1,0:T(8,128)(2,1)} copy(bf16[1,128,2048]{2,1,0:T(8,128)(2,1)} %bitcast.15) | data formatting | bytes 1048576
  161.2 0.0 copy-done.1
  161.2 0.7 copy.23
  161.9 0.0 copy-done
  161.9 0.7 copy.24
Async XLA Ops:
  157.4 3.8 %copy-start.1 = (bf16[128,512]{1,0:T(8,128)(2,1)S(1)}, bf16[128,512]{1,0:T(8,128)(2,1)}, u32[]{:S(2)}) copy-start(bf16[128,512]{1,0:T(8,128)(2,1)} %get-tuple-element.22) | copy-start | bytes 393220
  157.4 4.5 %copy-start = (bf16[128,512]{1,0:T(8,128)(2,1)S(1)}, bf16[128,512]{1,0:T(8,128)(2,1)}, u32[]{:S(2)}) copy-start(bf16[128,512]{1,0:T(8,128)(2,1)} %get-tuple-element.23) | copy-start | bytes 393220

commit v2 on v1

v2 whole, which is shorter than its diff:
```python
import jax
import jax.numpy as jnp
from jax import lax
from jax.experimental import pallas as pl
from jax.experimental.pallas import tpu as pltpu
from jax.sharding import PartitionSpec as P

HEAD = 128
ROWS = 128
HALF = 64
GROUP = 4
RING = 8
CTX = GROUP * RING
TOKENS = CTX * ROWS
QROWS = 4 * HALF
BLOCK = 256
EPS = 1e-06
SCALE = HEAD**-0.5
BF = jnp.bfloat16
F32 = jnp.float32
MESH = pl.DeviceIdType.MESH
VMEM = pl.BlockSpec(memory_space=pltpu.VMEM)
ANY = pl.BlockSpec(memory_space=pl.ANY)


def place():
    me = lax.axis_index("ctx")
    z = me // GROUP
    m = me % GROUP
    x, c = m // 2, m % 2
    peers = (2 * x + (1 - c), 2 * (1 - x) + c, 2 * (1 - x) + (1 - c))
    return z, m, peers


def ctx_of(z, m):
    return {"ctx": ((z + RING) % RING) * GROUP + m}


def remote(src, dst, send, recv, target):
    return pltpu.make_async_remote_copy(
        src_ref=src,
        dst_ref=dst,
        send_sem=send,
        recv_sem=recv,
        device_id=target,
        device_id_type=MESH,
    )


def greet(targets):
    barrier = pltpu.get_barrier_semaphore()
    for target in targets:
        pl.semaphore_signal(barrier, inc=1, device_id=target, device_id_type=MESH)
    return lambda: pl.semaphore_wait(barrier, len(targets))


def dot_nt(a, b):
    return lax.dot_general(a, b, (((1,), (1,)), ((), ())), preferred_element_type=F32)


def dot_nn(a, b):
    return jnp.dot(a, b, preferred_element_type=F32)


def stretches(b):
    return pl.ds(b * (BLOCK // HALF), BLOCK // HALF)


def columns(i):
    return slice(i * HEAD, (i + 1) * HEAD)


def kernel(
    order, inverse, types_f, types_b, table, qf, kf, vf, qb, kb, vb, go, gate, gain,
    handed, query_grad, key_grad, value_grad,
    stage_q, stage_kv, in_qf, in_qb, in_go, in_kvf, in_kvb,
    ks, vs, kt, dk, dv, acc, acc_t, qs, gs, dgk, dgv, q_pick, g_pick,
    dkv, sums, landed, total, dkv_in, att, att_in, dq, dq_in, gated,
    a_send, a_recv, g_send, g_recv, r_send, r_recv, h_send, h_recv,
):
    z, m, peers = place()
    sections = lax.axis_size("pipe")
    after = {"pipe": (lax.axis_index("pipe") + 1) % sections}
    before = {"pipe": (lax.axis_index("pipe") + sections - 1) % sections}
    greeted = greet(
        [ctx_of(z, p) for p in peers]
        + [ctx_of(z + 1, m), ctx_of(z - 1, m), after, before]
    )
    started = []


    def exchange(t, source, target, slot):
        copies = []
        for d, p in enumerate(peers):
            copy = remote(
                source.at[p], target.at[slot], a_send.at[d, t], a_recv.at[d, t], ctx_of(z, p)
            )
            copy.start()
            copies.append(copy)
            started.append(copy)
        return copies

    def stage_keys(t, types, keys, values):
        kinds = lax.broadcasted_iota(jnp.int32, (table.shape[0], ROWS), 0)
        onehot = jnp.where(kinds == types[...], 1.0, 0.0).astype(BF)
        rows = lax.dot_general(
            onehot, table[...], (((0,), (0,)), ((), ())), preferred_element_type=F32
        )
        typed = (keys[...].astype(F32) + rows).astype(BF)
        for h in range(GROUP):
            for half in range(2):
                rows = slice(half * HALF, (half + 1) * HALF)
                stage_kv[t, h, 0, half] = typed[rows, columns(h)]
                stage_kv[t, h, 1, half] = values[rows, columns(h)]

    def stage_rows(t, source):
        for h in range(GROUP):
            for g in range(4):
                for half in range(2):
                    rows = slice(half * HALF, (half + 1) * HALF)
                    stage_q[t, h, half, g] = source[rows, columns(h * 4 + g)]

    stage_keys(1, types_b, kb, vb)
    greeted()
    kvb_copies = exchange(0, stage_kv.at[1], in_kvb, z * GROUP + m)
    in_kvb[z * GROUP + m] = stage_kv[1, m]
    stage_rows(1, qb)
    qb_copies = exchange(1, stage_q.at[1], in_qb, m)
    in_qb[m] = stage_q[1, m]
    stage_rows(2, go)
    go_copies = exchange(2, stage_q.at[2], in_go, m)
    in_go[m] = stage_q[2, m]
    stage_keys(0, types_f, kf, vf)
    kvf_copies = exchange(3, stage_kv.at[0], in_kvf, z * GROUP + m)
    in_kvf[z * GROUP + m] = stage_kv[0, m]
    stage_rows(0, qf)
    qf_copies = exchange(4, stage_q.at[0], in_qf, m)
    in_qf[m] = stage_q[0, m]

    def arrive(copies):
        for copy in copies:
            copy.wait_recv()


    moving = {}

    def spread(t, step):
        target = (in_kvf, in_kvb)[t]
        for lane, way in enumerate((1, -1)):
            if step > 1:
                moving[t, lane].wait_recv()
            chunk = ((z - way * (step - 1) + RING) % RING) * GROUP
            first, count = (0, GROUP) if step < RING // 2 else (2 * lane, 2)
            part = target.at[pl.ds(chunk + first, count)]
            copy = remote(
                part, part, g_send.at[t, lane, step - 1], g_recv.at[t, lane, step - 1],
                ctx_of(z + way, m),
            )
            copy.start()
            started.append(copy)
            moving[t, lane] = copy

    def gathered(t):
        for lane in range(2):
            moving[t, lane].wait_recv()

    arrive(kvb_copies)
    for step in range(1, RING // 2 + 1):
        spread(1, step)
    arrive(kvf_copies)
    spread(0, 1)
    gathered(1)
    arrive(qb_copies)
    arrive(go_copies)


    first = [order[2 * GROUP * z + 2 * i] for i in range(GROUP)]
    second = [order[2 * GROUP * z + 2 * i + 1] for i in range(GROUP)]
    low = [jnp.minimum(a, b) for a, b in zip(first, second)]
    low_half = [jnp.where(a < b, 0, 1) for a, b in zip(first, second)]
    quart = [a * HALF // BLOCK for a in low]
    last = TOKENS // BLOCK - 1
    stretch = [low, [2 * CTX - 1 - a for a in low]]
    span = [slice(i * QROWS, (i + 1) * QROWS) for i in range(GROUP)]
    row_in = lax.broadcasted_iota(jnp.int32, (QROWS, HEAD), 0) % HALF

    def shrink_rows(position):
        return lax.rsqrt((position * HALF + row_in + 1).astype(F32))

    def query_rows(source, i, w):
        half = low_half[i] if w == 0 else 1 - low_half[i]
        return source[i, half].reshape(QROWS, HEAD)

    def choice(i, n):
        is_low = n <= quart[i]
        return is_low, jnp.where(is_low, n, last - n), jnp.where(is_low, 0, 1)

    def bound_low(i, n):
        return jnp.where(n == quart[i], low[i] * HALF - n * BLOCK, BLOCK)

    def bound_high(i):
        return stretch[1][i] * HALF - (last - quart[i]) * BLOCK

    def put_rows(target, i, low_rows, high_rows):
        shape = (4, HALF, HEAD)
        a, b = low_rows.astype(BF).reshape(shape), high_rows.astype(BF).reshape(shape)
        target[i, 0] = jnp.where(low_half[i] == 0, a, b)
        target[i, 1] = jnp.where(low_half[i] == 0, b, a)

    def unsort(source):
        def fill(b, _):
            for k in range(BLOCK // HALF):
                j = inverse[b * (BLOCK // HALF) + k]
                ks[b, k * HALF : (k + 1) * HALF] = source[j // 2, 0, j % 2]
                vs[b, k * HALF : (k + 1) * HALF] = source[j // 2, 1, j % 2]
            return 0

        lax.fori_loop(0, last + 1, fill, 0)


    unsort(in_kvb)

    def turn(b, _):
        kt[b] = ks[b].T
        return 0

    lax.fori_loop(0, last + 1, turn, 0)
    for i in range(GROUP):
        for w in range(2):
            qs[w, i] = query_rows(in_qb, i, w)
            g = query_rows(in_go, i, w).astype(F32) * shrink_rows(stretch[w][i])
            gs[w, i] = g.astype(BF)
    key_over = lax.broadcasted_iota(jnp.int32, (BLOCK, QROWS), 0) - (
        lax.broadcasted_iota(jnp.int32, (BLOCK, QROWS), 1) % HALF
    )

    def slopes(k, v, q, g):
        u = dot_nt(k, q) * (0.5 * SCALE)
        grad = dot_nt(v, g)
        t = jnp.tanh(u)
        ut = u * t
        return u + ut, (0.5 + 0.5 * t) * (1.0 + (u - ut)) * grad

    def seen(over, bound, value):
        return jnp.where(over <= bound, value, 0.0).astype(BF)

    def backward_full(b, _):
        q, g = qs[1].reshape(GROUP * QROWS, HEAD), gs[1].reshape(GROUP * QROWS, HEAD)
        p, s = slopes(ks[b], vs[b], q, g)
        p = p.astype(BF)
        s = s.astype(BF)
        dv[stretches(b)] = dot_nn(p, g).reshape(-1, HALF, HEAD)
        dk[stretches(b)] = dot_nn(s, q).reshape(-1, HALF, HEAD)
        acc_t[1] += dot_nn(kt[b], s)
        return 0

    def backward_edge(i):
        at = last - quart[i]
        q, g = qs[1, i], gs[1, i]
        p, s = slopes(ks[at], vs[at], q, g)
        p = seen(key_over, bound_high(i), p)
        s = seen(key_over, bound_high(i), s)
        dgv[i] = dot_nn(p, g)
        dgk[i] = dot_nn(s, q)
        acc_t[1, :, span[i]] += dot_nn(kt[at], s)

    def backward_choice(n, _):
        zero = jnp.zeros((QROWS, HEAD), BF)
        ps, ss = [], []
        for i in range(GROUP):
            is_low, at, w = choice(i, n)
            q, g = qs[w, i], gs[w, i]
            p, s = slopes(ks[at], vs[at], q, g)
            p = seen(key_over, bound_low(i, n), p)
            s = seen(key_over, bound_low(i, n), s)
            part = dot_nn(kt[at], s)
            acc_t[0, :, span[i]] += jnp.where(is_low, part, 0.0)
            acc_t[1, :, span[i]] += jnp.where(is_low, 0.0, part)
            g_pick[span[i], :HEAD] = jnp.where(is_low, g, zero)
            g_pick[span[i], HEAD:] = jnp.where(is_low, zero, g)
            q_pick[span[i], :HEAD] = jnp.where(is_low, q, zero)
            q_pick[span[i], HEAD:] = jnp.where(is_low, zero, q)
            ps.append(p)
            ss.append(s)
        both_v = dot_nn(jnp.concatenate(ps, 1), g_pick[...])
        both_k = dot_nn(jnp.concatenate(ss, 1), q_pick[...])
        dv[stretches(n)] += both_v[:, :HEAD].reshape(-1, HALF, HEAD)
        dk[stretches(n)] += both_k[:, :HEAD].reshape(-1, HALF, HEAD)
        high_v, high_k = both_v[:, HEAD:], both_k[:, HEAD:]
        for i in range(GROUP):
            here = jnp.where(n == quart[i], 1.0, 0.0)
            high_v += dgv[i] * here
            high_k += dgk[i] * here
        dv[stretches(last - n)] = high_v.reshape(-1, HALF, HEAD)
        dk[stretches(last - n)] = high_k.reshape(-1, HALF, HEAD)
        return 0

    half_blocks = (last + 1) // 2
    middle = half_blocks // 2
    acc_t[...] = jnp.zeros_like(acc_t)
    lax.fori_loop(0, middle, backward_full, 0)
    spread(0, 2)
    lax.fori_loop(middle, half_blocks, backward_full, 0)
    for i in range(GROUP):
        backward_edge(i)
    spread(0, 3)
    lax.fori_loop(0, middle, backward_choice, 0)
    spread(0, 4)
    lax.fori_loop(middle, half_blocks, backward_choice, 0)


    def store_chunk(distance):
        chunk = ((z + distance + RING) % RING) * GROUP

        def store(c, _):
            for half in range(2):
                p = order[2 * (chunk + c) + half]
                dkv[chunk + c, 0, half] = (dk[p] * SCALE).astype(BF)
                dkv[chunk + c, 1, half] = dv[p].astype(BF)
            return 0

        lax.fori_loop(0, GROUP, store, 0)

    reducing = {}

    def reduce(step, lane, part):
        way = (1, -1)[lane]
        chunk = ((z + way * (RING // 2 - step) + RING) % RING) * GROUP
        mine = pl.ds(chunk + 2 * part, 2)
        if step == 0 or (step == 1 and part != lane):
            source = dkv.at[mine]
        else:
            reducing[lane, part].wait_recv()
            arrived = landed[lane, step - 1, part].astype(F32)
            sums[lane, step - 1, part] = (dkv[mine].astype(F32) + arrived).astype(BF)
            source = sums.at[lane, step - 1, part]
        copy = remote(
            source, landed.at[lane, step, part],
            r_send.at[lane, step, part], r_recv.at[lane, step, part], ctx_of(z + way, m),
        )
        copy.start()
        started.append(copy)
        reducing[lane, part] = copy

    def reduce_all(step):
        for part in range(2):
            for lane in range(2):
                reduce(step, lane, part)

    store_chunk(RING // 2)
    for lane in range(2):
        reduce(0, lane, lane)
    for distance in (3, -3):
        store_chunk(distance)
    for lane in range(2):
        reduce(1, lane, 1 - lane)
    for i in range(GROUP):
        put_rows(
            dq, i, (acc_t[0, :, span[i]] * SCALE).T, (acc_t[1, :, span[i]] * SCALE).T
        )
    dq_copies = exchange(5, dq, dq_in, m)
    dq_in[m] = dq[m]
    for distance in (2, -2, 1, -1, 0):
        store_chunk(distance)


    gathered(0)
    arrive(qf_copies)
    unsort(in_kvf)
    for i in range(GROUP):
        for w in range(2):
            qs[w, i] = query_rows(in_qf, i, w)
    query_over = lax.broadcasted_iota(jnp.int32, (QROWS, BLOCK), 1) - (
        lax.broadcasted_iota(jnp.int32, (QROWS, BLOCK), 0) % HALF
    )

    def weigh(q, k):
        u = dot_nt(q, k) * (0.5 * SCALE)
        return u + u * jnp.tanh(u)

    def forward_full(b, _):
        q = qs[1].reshape(GROUP * QROWS, HEAD)
        acc[1] += dot_nn(weigh(q, ks[b]).astype(BF), vs[b])
        return 0

    def forward_choice(n, _):
        for i in range(GROUP):
            is_low, at, w = choice(i, n)
            p = seen(query_over, bound_low(i, n), weigh(qs[w, i], ks[at]))
            part = dot_nn(p, vs[at])
            acc[0, span[i]] += jnp.where(is_low, part, 0.0)
            acc[1, span[i]] += jnp.where(is_low, 0.0, part)
        return 0

    acc[...] = jnp.zeros_like(acc)
    lax.fori_loop(0, middle, forward_full, 0)
    for lane in range(2):
        reduce(1, lane, lane)
    lax.fori_loop(middle, half_blocks, forward_full, 0)
    for i in range(GROUP):
        at = last - quart[i]
        p = seen(query_over, bound_high(i), weigh(qs[1, i], ks[at]))
        acc[1, span[i]] += dot_nn(p, vs[at])
    lax.fori_loop(0, middle, forward_choice, 0)
    reduce_all(2)
    lax.fori_loop(middle, half_blocks, forward_choice, 0)
    for i in range(GROUP):
        put_rows(
            att, i,
            acc[0, span[i]] * shrink_rows(stretch[0][i]),
            acc[1, span[i]] * shrink_rows(stretch[1][i]),
        )
    att_copies = exchange(6, att, att_in, m)
    att_in[m] = att[m]
    reduce_all(3)


    arrive(att_copies)
    for half in range(2):
        rows = slice(half * HALF, (half + 1) * HALF)
        squares = jnp.zeros((HALF, HEAD), F32)
        for h in range(GROUP):
            for g in range(4):
                part = att_in[h, half, g].astype(F32)
                squares += part * part
        mean = jnp.sum(squares, axis=1, keepdims=True) * (1.0 / (16 * HEAD))
        factor = lax.rsqrt(mean + EPS)
        for h in range(GROUP):
            for g in range(4):
                cols = columns(h * 4 + g)
                gated[rows, cols] = (
                    att_in[h, half, g].astype(F32)
                    * factor * gain[:, cols] * gate[rows, cols].astype(F32)
                ).astype(BF)
    hand = remote(gated, handed, h_send, h_recv, after)
    hand.start()

    arrive(dq_copies)
    for h in range(GROUP):
        for g in range(4):
            for half in range(2):
                rows = slice(half * HALF, (half + 1) * HALF)
                query_grad[rows, columns(h * 4 + g)] = dq_in[h, half, g]
    for part in range(2):
        for lane in range(2):
            reducing[lane, part].wait_recv()
        mine = pl.ds(z * GROUP + 2 * part, 2)
        total[2 * part : 2 * part + 2] = (
            dkv[mine].astype(F32)
            + landed[0, RING // 2 - 1, part].astype(F32)
            + landed[1, RING // 2 - 1, part].astype(F32)
        ).astype(BF)
    kv_copies = exchange(7, total, dkv_in, m)
    dkv_in[m] = total[m]
    arrive(kv_copies)
    for h in range(GROUP):
        for half in range(2):
            rows = slice(half * HALF, (half + 1) * HALF)
            key_grad[rows, columns(h)] = dkv_in[h, 0, half]
            value_grad[rows, columns(h)] = dkv_in[h, 1, half]
    for copy in started:
        copy.wait_send()
    hand.wait()


def body(
    query_fwd, key_fwd, value_fwd, gate_fwd, types_fwd,
    query_bwd, key_bwd, value_bwd, grad_out, types_bwd,
    type_key, norm_gain, stretch_order,
):
    order = stretch_order[0]
    slots = jnp.arange(order.shape[0], dtype=jnp.int32)
    inverse = jnp.sum(
        jnp.where(order[None, :] == slots[:, None], slots[None, :], 0), axis=1
    ).astype(jnp.int32)
    dma = pltpu.SemaphoreType.DMA
    wide, narrow = (ROWS, 16 * HEAD), (ROWS, GROUP * HEAD)
    smem = pl.BlockSpec(memory_space=pltpu.SMEM)
    part = (HALF, HEAD)
    blocks = TOKENS // BLOCK
    heads, pairs = (GROUP, 2, 4, *part), (CTX, 2, 2, *part)
    handed, query_grad, key_grad, value_grad = pl.pallas_call(
        kernel,
        out_shape=(
            jax.ShapeDtypeStruct(wide, BF),
            jax.ShapeDtypeStruct(wide, BF),
            jax.ShapeDtypeStruct(narrow, BF),
            jax.ShapeDtypeStruct(narrow, BF),
        ),
        in_specs=[smem, smem] + [VMEM] * 12,
        out_specs=(ANY, VMEM, VMEM, VMEM),
        scratch_shapes=[
            pltpu.VMEM((3, *heads), BF),
            pltpu.VMEM((2, GROUP, 2, 2, *part), BF),
            pltpu.VMEM(heads, BF),
            pltpu.VMEM(heads, BF),
            pltpu.VMEM(heads, BF),
            pltpu.VMEM(pairs, BF),
            pltpu.VMEM(pairs, BF),
            pltpu.VMEM((blocks, BLOCK, HEAD), BF),
            pltpu.VMEM((blocks, BLOCK, HEAD), BF),
            pltpu.VMEM((blocks, HEAD, BLOCK), BF),
            pltpu.VMEM((2 * CTX, *part), F32),
            pltpu.VMEM((2 * CTX, *part), F32),
            pltpu.VMEM((2, GROUP * QROWS, HEAD), F32),
            pltpu.VMEM((2, HEAD, GROUP * QROWS), F32),
            pltpu.VMEM((2, GROUP, QROWS, HEAD), BF),
            pltpu.VMEM((2, GROUP, QROWS, HEAD), BF),
            pltpu.VMEM((GROUP, BLOCK, HEAD), F32),
            pltpu.VMEM((GROUP, BLOCK, HEAD), F32),
            pltpu.VMEM((GROUP * QROWS, 2 * HEAD), BF),
            pltpu.VMEM((GROUP * QROWS, 2 * HEAD), BF),
            pltpu.VMEM(pairs, BF),
            pltpu.VMEM((2, RING // 2 - 1, 2, 2, 2, 2, *part), BF),
            pltpu.VMEM((2, RING // 2, 2, 2, 2, 2, *part), BF),
            pltpu.VMEM((GROUP, 2, 2, *part), BF),
            pltpu.VMEM((GROUP, 2, 2, *part), BF),
            pltpu.VMEM(heads, BF),
            pltpu.VMEM(heads, BF),
            pltpu.VMEM(heads, BF),
            pltpu.VMEM(heads, BF),
            pltpu.VMEM(wide, BF),
            dma((3, 8)),
            dma((3, 8)),
            dma((2, 2, RING // 2)),
            dma((2, 2, RING // 2)),
            dma((2, RING // 2, 2)),
            dma((2, RING // 2, 2)),
            dma,
            dma,
        ],
        compiler_params=pltpu.CompilerParams(
            collective_id=0, has_side_effects=True, vmem_limit_bytes=56 * 1024 * 1024
        ),
        name="attention",
    )(
        order, inverse, types_fwd, types_bwd, type_key[0],
        query_fwd[0], key_fwd[0], value_fwd[0],
        query_bwd[0], key_bwd[0], value_bwd[0], grad_out[0], gate_fwd[0], norm_gain,
    )
    return handed[None], query_grad[None], key_grad[None], value_grad[None]


def solution(mesh):
    rows = P("pipe", "ctx", None)
    section = P("pipe", None)
    types = P("pipe", "ctx")
    return jax.shard_map(
        body,
        mesh=mesh,
        in_specs=(
            rows, rows, rows, rows, types, rows, rows, rows, rows, types,
            P("pipe", None, None), section, section,
        ),
        out_specs=(rows, rows, rows, rows),
        check_vma=False,
    )
```

time: 163 us -> 117 us (0.72)
  Pallas kernels: 157 us -> 110 us
    pallas_call x3 -> x1, Pallas kernels: 157 us -> 110 us  [body(): pl.pallas_call(kernel, out_shape=(jax.ShapeDtypeStruct(wide, BF), jax.Sha...]
    unnamed x8 -> x12, local copies, waits for them, and re-layouts: 5.12 us -> 5.22 us
where the time goes in v2:
time: 117 us
  Pallas kernels  110 us (94%)
  local copies, waits for them, and re-layouts  5.22 us (4%)
    pallas_call x1, Pallas kernels, body(): pl.pallas_call(kernel, out_shape=(jax.ShapeDtypeStruct(wide, BF), jax.Sha...  110 us
    unnamed x12, local copies, waits for them, and re-layouts  5.22 us

profile of v2, /device:TPU:1, one launch (start us, length us, event | category | flops | bytes accessed | tf_op | source)
XLA Modules:
  0.0 116.7 jit_solution(11698299440072936750)
XLA Ops:
  0.6 0.0 copy-start.3
  0.6 0.6 copy-done.3
  1.3 0.6 select_reduce_fusion.inverse
  1.9 110.2 %attention.1 = (bf16[128,2048]{1,0:T(8,128)(2,1)}, bf16[128,2048]{1,0:T(8,128)(2,1)}, bf16[128,512]{1,0:T(8,128)(2,1)}, bf16[128,512]{1,0:T(8,128)(2,1)}) custom-call(s32[64]{0:T(128)} %bitcast.27, s32[64]{0:T(128)} %select_reduce_fusion.inverse, s32[1,128]{1,0:T(1,128)} %types_f.1, s32[1,128]{1,0:T(1,128)} %types_b.1, bf16[64,512]{1,0:T(8,128)(2,1)} %bitcast.26, ...), custom_call_target="tpu_custom_call" | custom-call | tf_op jit(solution)/shard_map/attention/pallas_call | solution.py:482
  112.1 0.0 copy-start
  112.1 1.9 %copy.21 = bf16[1,128,2048]{2,1,0:T(8,128)(2,1)} copy(bf16[1,128,2048]{2,1,0:T(8,128)(2,1)} %bitcast.15) | data formatting | bytes 1048576
  114.0 0.0 copy-done
  114.0 0.0 copy-start.2
  114.0 0.8 copy.22
  114.8 0.2 copy-done.2
  115.1 0.0 copy-start.1
  115.1 0.7 copy.23
  115.7 0.3 copy-done.1
  116.0 0.7 copy.24
Async XLA Ops:
  0.6 0.7 copy-start.3
  112.1 2.0 %copy-start = (bf16[128,2048]{1,0:T(8,128)(2,1)S(1)}, bf16[128,2048]{1,0:T(8,128)(2,1)}, u32[]{:S(2)}) copy-start(bf16[128,2048]{1,0:T(8,128)(2,1)} %get-tuple-element.9) | copy-start | bytes 1572868
  114.0 1.0 copy-start.2
  115.1 1.0 copy-start.1

commit v3 on v2

--- a/solution.py
+++ b/solution.py
@@ -20,7 +20,6 @@
 F32 = jnp.float32
 MESH = pl.DeviceIdType.MESH
 VMEM = pl.BlockSpec(memory_space=pltpu.VMEM)
-ANY = pl.BlockSpec(memory_space=pl.ANY)
 
 
 def place():
@@ -71,20 +70,31 @@
 
 
 def kernel(
-    order, inverse, types_f, types_b, table, qf, kf, vf, qb, kb, vb, go, gate, gain,
+    order, types_f, types_b, table, qf, kf, vf, qb, kb, vb, go, gate, gain,
     handed, query_grad, key_grad, value_grad,
-    stage_q, stage_kv, in_qf, in_qb, in_go, in_kvf, in_kvb,
+    inverse, stage_q, stage_kv, in_qf, in_qb, in_go, in_gate, in_kvf, in_kvb,
     ks, vs, kt, dk, dv, acc, acc_t, qs, gs, dgk, dgv, q_pick, g_pick,
-    dkv, sums, landed, total, dkv_in, att, att_in, dq, dq_in, gated,
-    a_send, a_recv, g_send, g_recv, r_send, r_recv, h_send, h_recv,
+    dkv, sums, landed, total, dkv_in, att, norms, norms_in, dq, dq_in, gated, hand_in,
+    a_send, a_recv, b_send, b_recv, g_send, g_recv, r_send, r_recv,
+    n_send, n_recv, h_send, h_recv,
 ):
     z, m, peers = place()
+    x = m // 2
+    members = (m, *peers)
+    chips = (2 * x, 2 * (1 - x))
     sections = lax.axis_size("pipe")
-    after = {"pipe": (lax.axis_index("pipe") + 1) % sections}
-    before = {"pipe": (lax.axis_index("pipe") + sections - 1) % sections}
+    section = lax.axis_index("pipe")
+
+    def beside(distance, member):
+        return {
+            "pipe": (section + distance + sections) % sections,
+            "ctx": z * GROUP + member,
+        }
+
     greeted = greet(
         [ctx_of(z, p) for p in peers]
-        + [ctx_of(z + 1, m), ctx_of(z - 1, m), after, before]
+        + [ctx_of(z + 1, m), ctx_of(z - 1, m)]
+        + [beside(d, s) for d in (1, -1) for s in range(GROUP)]
     )
     started = []
 
@@ -120,55 +130,90 @@
                     rows = slice(half * HALF, (half + 1) * HALF)
                     stage_q[t, h, half, g] = source[rows, columns(h * 4 + g)]
 
+    def arrive(copies):
+        for copy in copies:
+            copy.wait_recv()
+
+
+    moving = {}
+
+    def ring_hop(t, target, first, count, step, lane, part, send, recv):
+        way = (1, -1)[lane]
+        if step > 1:
+            moving[t, lane, part].wait_recv()
+        chunk = ((z - way * (step - 1) + RING) % RING) * GROUP
+        view = target.at[pl.ds(chunk + first, count)]
+        copy = remote(
+            view, view, send.at[lane, step - 1, part], recv.at[lane, step - 1, part],
+            ctx_of(z + way, m),
+        )
+        copy.start()
+        started.append(copy)
+        moving[t, lane, part] = copy
+
+    def spread_b(step, d):
+        for lane in range(2):
+            if step < RING // 2 or d % 2 == lane:
+                ring_hop(1, in_kvb, members[d], 1, step, lane, d, b_send, b_recv)
+
+    def spread_f(step, part):
+        for lane in range(2):
+            if step < RING // 2 or part == lane:
+                ring_hop(0, in_kvf, chips[part], 2, step, lane, part, g_send, g_recv)
+
+    def gathered(t):
+        for (kind, _, _), copy in moving.items():
+            if kind == t:
+                copy.wait_recv()
+
+    def invert(first, count):
+        def one(p, _):
+            slot = 0
+            for j in range(2 * CTX):
+                slot = jnp.maximum(slot, jnp.where(order[j] == p, j, 0))
+            inverse[p] = slot
+            inverse[2 * CTX - 1 - p] = slot + 1 - 2 * (slot % 2)
+            return 0
+
+        lax.fori_loop(first, first + count, one, 0)
+
     stage_keys(1, types_b, kb, vb)
     greeted()
     kvb_copies = exchange(0, stage_kv.at[1], in_kvb, z * GROUP + m)
     in_kvb[z * GROUP + m] = stage_kv[1, m]
+    spread_b(1, 0)
     stage_rows(1, qb)
     qb_copies = exchange(1, stage_q.at[1], in_qb, m)
+    kvb_copies[0].wait_recv()
+    spread_b(1, 1)
     in_qb[m] = stage_q[1, m]
     stage_rows(2, go)
     go_copies = exchange(2, stage_q.at[2], in_go, m)
     in_go[m] = stage_q[2, m]
+    for d in (1, 2):
+        kvb_copies[d].wait_recv()
+        spread_b(1, d + 1)
     stage_keys(0, types_f, kf, vf)
+    spread_b(2, 0)
     kvf_copies = exchange(3, stage_kv.at[0], in_kvf, z * GROUP + m)
     in_kvf[z * GROUP + m] = stage_kv[0, m]
+    spread_b(2, 1)
     stage_rows(0, qf)
     qf_copies = exchange(4, stage_q.at[0], in_qf, m)
     in_qf[m] = stage_q[0, m]
-
-    def arrive(copies):
-        for copy in copies:
-            copy.wait_recv()
-
-
-    moving = {}
-
-    def spread(t, step):
-        target = (in_kvf, in_kvb)[t]
-        for lane, way in enumerate((1, -1)):
-            if step > 1:
-                moving[t, lane].wait_recv()
-            chunk = ((z - way * (step - 1) + RING) % RING) * GROUP
-            first, count = (0, GROUP) if step < RING // 2 else (2 * lane, 2)
-            part = target.at[pl.ds(chunk + first, count)]
-            copy = remote(
-                part, part, g_send.at[t, lane, step - 1], g_recv.at[t, lane, step - 1],
-                ctx_of(z + way, m),
-            )
-            copy.start()
-            started.append(copy)
-            moving[t, lane] = copy
-
-    def gathered(t):
-        for lane in range(2):
-            moving[t, lane].wait_recv()
-
-    arrive(kvb_copies)
-    for step in range(1, RING // 2 + 1):
-        spread(1, step)
+    spread_b(2, 2)
+    stage_rows(3, gate)
+    gate_copies = exchange(6, stage_q.at[3], in_gate, m)
+    in_gate[m] = stage_q[3, m]
+    spread_b(2, 3)
+    for d in range(GROUP):
+        invert(d * CTX // GROUP, CTX // GROUP)
+        spread_b(3, d)
+    for d in range(GROUP):
+        spread_b(4, d)
     arrive(kvf_copies)
-    spread(0, 1)
+    for part in range(2):
+        spread_f(1, part)
     gathered(1)
     arrive(qb_copies)
     arrive(go_copies)
@@ -298,15 +343,19 @@
     half_blocks = (last + 1) // 2
     middle = half_blocks // 2
     acc_t[...] = jnp.zeros_like(acc_t)
-    lax.fori_loop(0, middle, backward_full, 0)
-    spread(0, 2)
-    lax.fori_loop(middle, half_blocks, backward_full, 0)
+    spread_f(2, 0)
+    lax.fori_loop(0, 3, backward_full, 0)
+    spread_f(2, 1)
+    lax.fori_loop(3, 6, backward_full, 0)
+    spread_f(3, 0)
+    lax.fori_loop(6, half_blocks, backward_full, 0)
     for i in range(GROUP):
         backward_edge(i)
-    spread(0, 3)
-    lax.fori_loop(0, middle, backward_choice, 0)
-    spread(0, 4)
-    lax.fori_loop(middle, half_blocks, backward_choice, 0)
+    spread_f(3, 1)
+    lax.fori_loop(0, 2, backward_choice, 0)
+    for part in range(2):
+        spread_f(4, part)
+    lax.fori_loop(2, half_blocks, backward_choice, 0)
 
 
     def store_chunk(distance):
@@ -326,7 +375,7 @@
     def reduce(step, lane, part):
         way = (1, -1)[lane]
         chunk = ((z + way * (RING // 2 - step) + RING) % RING) * GROUP
-        mine = pl.ds(chunk + 2 * part, 2)
+        mine = pl.ds(chunk + chips[part], 2)
         if step == 0 or (step == 1 and part != lane):
             source = dkv.at[mine]
         else:
@@ -342,18 +391,19 @@
         started.append(copy)
         reducing[lane, part] = copy
 
-    def reduce_all(step):
-        for part in range(2):
-            for lane in range(2):
-                reduce(step, lane, part)
+    def reduce_fresh(step):
+        for lane in range(2):
+            reduce(step, lane, 1 - lane)
+
+    def reduce_chained(step):
+        for lane in range(2):
+            reduce(step, lane, lane)
 
     store_chunk(RING // 2)
-    for lane in range(2):
-        reduce(0, lane, lane)
+    reduce_chained(0)
     for distance in (3, -3):
         store_chunk(distance)
-    for lane in range(2):
-        reduce(1, lane, 1 - lane)
+    reduce_fresh(1)
     for i in range(GROUP):
         put_rows(
             dq, i, (acc_t[0, :, span[i]] * SCALE).T, (acc_t[1, :, span[i]] * SCALE).T
@@ -378,89 +428,136 @@
         u = dot_nt(q, k) * (0.5 * SCALE)
         return u + u * jnp.tanh(u)
 
-    def forward_full(b, _):
-        q = qs[1].reshape(GROUP * QROWS, HEAD)
-        acc[1] += dot_nn(weigh(q, ks[b]).astype(BF), vs[b])
-        return 0
-
-    def forward_choice(n, _):
-        for i in range(GROUP):
-            is_low, at, w = choice(i, n)
-            p = seen(query_over, bound_low(i, n), weigh(qs[w, i], ks[at]))
-            part = dot_nn(p, vs[at])
-            acc[0, span[i]] += jnp.where(is_low, part, 0.0)
-            acc[1, span[i]] += jnp.where(is_low, 0.0, part)
-        return 0
+    def forward_full(part):
+        pairs = slice(2 * part, 2 * part + 2)
+        rows = slice(2 * part * QROWS, 2 * (part + 1) * QROWS)
+
+        def step(b, _):
+            q = qs[1, pairs].reshape(2 * QROWS, HEAD)
+            acc[1, rows] += dot_nn(weigh(q, ks[b]).astype(BF), vs[b])
+            return 0
+
+        lax.fori_loop(0, half_blocks, step, 0)
+
+    def forward_edge(part):
+        for i in (2 * part, 2 * part + 1):
+            at = last - quart[i]
+            p = seen(query_over, bound_high(i), weigh(qs[1, i], ks[at]))
+            acc[1, span[i]] += dot_nn(p, vs[at])
+
+    def forward_choice(part, first, end):
+        def step(n, _):
+            for i in (2 * part, 2 * part + 1):
+                is_low, at, w = choice(i, n)
+                p = seen(query_over, bound_low(i, n), weigh(qs[w, i], ks[at]))
+                out = dot_nn(p, vs[at])
+                acc[0, span[i]] += jnp.where(is_low, out, 0.0)
+                acc[1, span[i]] += jnp.where(is_low, 0.0, out)
+            return 0
+
+        lax.fori_loop(first, end, step, 0)
+
+
+    norm_copies = [[], []]
+
+    def measure_rows(part):
+        for i in (2 * part, 2 * part + 1):
+            shape = (4, HALF, HEAD)
+            low_rows = (acc[0, span[i]] * shrink_rows(stretch[0][i])).reshape(shape)
+            high_rows = (acc[1, span[i]] * shrink_rows(stretch[1][i])).reshape(shape)
+            att[i, 0] = jnp.where(low_half[i] == 0, low_rows, high_rows)
+            att[i, 1] = jnp.where(low_half[i] == 0, high_rows, low_rows)
+            rows = att[i]
+            square = jnp.sum(rows * rows, axis=1).reshape(ROWS, HEAD)
+            square = jnp.sum(square, axis=1, keepdims=True)
+            norms[i] = jnp.broadcast_to(square, (ROWS, HEAD)).T[:8]
+        pairs = pl.ds(2 * part, 2)
+        for d, p in enumerate(peers):
+            copy = remote(
+                norms.at[pairs], norms_in.at[d, pairs],
+                n_send.at[d, part], n_recv.at[d, part], ctx_of(z, p),
+            )
+            copy.start()
+            started.append(copy)
+            norm_copies[part].append(copy)
+
+    def hand_rows(part):
+        arrive(norm_copies[part])
+        for i in (2 * part, 2 * part + 1):
+            row = norms[i] + norms_in[0, i] + norms_in[1, i] + norms_in[2, i]
+            square = jnp.broadcast_to(row[:1], (HEAD, ROWS)).T
+            factor = lax.rsqrt(square * (1.0 / (16 * HEAD)) + EPS).reshape(2, 1, HALF, HEAD)
+            for g in range(4):
+                cols = pl.ds(pl.multiple_of((m * 4 + g) * HEAD, HEAD), HEAD)
+                gated[i, :, g] = (
+                    att[i, :, g] * factor[:, 0]
+                    * gain[:, cols].reshape(1, 1, HEAD)
+                    * in_gate[i, :, g].astype(F32)
+                ).astype(BF)
+            copy = remote(
+                gated.at[i], hand_in.at[m], h_send.at[i], h_recv.at[m], beside(1, i)
+            )
+            copy.start()
+            started.append(copy)
 
     acc[...] = jnp.zeros_like(acc)
-    lax.fori_loop(0, middle, forward_full, 0)
-    for lane in range(2):
-        reduce(1, lane, lane)
-    lax.fori_loop(middle, half_blocks, forward_full, 0)
-    for i in range(GROUP):
-        at = last - quart[i]
-        p = seen(query_over, bound_high(i), weigh(qs[1, i], ks[at]))
-        acc[1, span[i]] += dot_nn(p, vs[at])
-    lax.fori_loop(0, middle, forward_choice, 0)
-    reduce_all(2)
-    lax.fori_loop(middle, half_blocks, forward_choice, 0)
-    for i in range(GROUP):
-        put_rows(
-            att, i,
-            acc[0, span[i]] * shrink_rows(stretch[0][i]),
-            acc[1, span[i]] * shrink_rows(stretch[1][i]),
-        )
-    att_copies = exchange(6, att, att_in, m)
-    att_in[m] = att[m]
-    reduce_all(3)
-
-
-    arrive(att_copies)
-    for half in range(2):
-        rows = slice(half * HALF, (half + 1) * HALF)
-        squares = jnp.zeros((HALF, HEAD), F32)
-        for h in range(GROUP):
-            for g in range(4):
-                part = att_in[h, half, g].astype(F32)
-                squares += part * part
-        mean = jnp.sum(squares, axis=1, keepdims=True) * (1.0 / (16 * HEAD))
-        factor = lax.rsqrt(mean + EPS)
-        for h in range(GROUP):
-            for g in range(4):
-                cols = columns(h * 4 + g)
-                gated[rows, cols] = (
-                    att_in[h, half, g].astype(F32)
-                    * factor * gain[:, cols] * gate[rows, cols].astype(F32)
-                ).astype(BF)
-    hand = remote(gated, handed, h_send, h_recv, after)
-    hand.start()
-
+    forward_full(0)
+    reduce_chained(1)
+    forward_edge(0)
+    forward_choice(0, 0, middle)
+    reduce_fresh(2)
+    forward_choice(0, middle, half_blocks)
+    measure_rows(0)
+    reduce_chained(2)
+    forward_full(1)
+    reduce_fresh(3)
+    arrive(gate_copies)
+    hand_rows(0)
+    forward_edge(1)
+    forward_choice(1, 0, middle)
+    reduce_chained(3)
+    forward_choice(1, middle, half_blocks)
+    measure_rows(1)
     arrive(dq_copies)
     for h in range(GROUP):
         for g in range(4):
             for half in range(2):
                 rows = slice(half * HALF, (half + 1) * HALF)
                 query_grad[rows, columns(h * 4 + g)] = dq_in[h, half, g]
-    for part in range(2):
+    hand_rows(1)
+
+
+    for part in (1, 0):
         for lane in range(2):
             reducing[lane, part].wait_recv()
-        mine = pl.ds(z * GROUP + 2 * part, 2)
-        total[2 * part : 2 * part + 2] = (
-            dkv[mine].astype(F32)
+        total[pl.ds(chips[part], 2)] = (
+            dkv[pl.ds(z * GROUP + chips[part], 2)].astype(F32)
             + landed[0, RING // 2 - 1, part].astype(F32)
             + landed[1, RING // 2 - 1, part].astype(F32)
         ).astype(BF)
-    kv_copies = exchange(7, total, dkv_in, m)
+        for d in ((1, 2), (0,))[1 - part]:
+            copy = remote(
+                total.at[peers[d]], dkv_in.at[m], a_send.at[d, 7], a_recv.at[d, 7],
+                ctx_of(z, peers[d]),
+            )
+            copy.start()
+            started.append(copy)
+            moving[2, 0, d] = copy
     dkv_in[m] = total[m]
-    arrive(kv_copies)
+    gathered(2)
     for h in range(GROUP):
         for half in range(2):
             rows = slice(half * HALF, (half + 1) * HALF)
             key_grad[rows, columns(h)] = dkv_in[h, 0, half]
             value_grad[rows, columns(h)] = dkv_in[h, 1, half]
+    for h in range(GROUP):
+        remote(gated.at[h], hand_in.at[h], h_send.at[h], h_recv.at[h], beside(1, h)).wait_recv()
+        for g in range(4):
+            for half in range(2):
+                rows = slice(half * HALF, (half + 1) * HALF)
+                handed[rows, columns(h * 4 + g)] = hand_in[h, half, g]
     for copy in started:
         copy.wait_send()
-    hand.wait()
 
 
 def body(
@@ -469,10 +566,6 @@
     type_key, norm_gain, stretch_order,
 ):
     order = stretch_order[0]
-    slots = jnp.arange(order.shape[0], dtype=jnp.int32)
-    inverse = jnp.sum(
-        jnp.where(order[None, :] == slots[:, None], slots[None, :], 0), axis=1
-    ).astype(jnp.int32)
     dma = pltpu.SemaphoreType.DMA
     wide, narrow = (ROWS, 16 * HEAD), (ROWS, GROUP * HEAD)
     smem = pl.BlockSpec(memory_space=pltpu.SMEM)
@@ -487,11 +580,13 @@
             jax.ShapeDtypeStruct(narrow, BF),
             jax.ShapeDtypeStruct(narrow, BF),
         ),
-        in_specs=[smem, smem] + [VMEM] * 12,
-        out_specs=(ANY, VMEM, VMEM, VMEM),
+        in_specs=[smem] + [VMEM] * 12,
+        out_specs=(VMEM,) * 4,
         scratch_shapes=[
-            pltpu.VMEM((3, *heads), BF),
+            pltpu.SMEM((2 * CTX,), jnp.int32),
+            pltpu.VMEM((4, *heads), BF),
             pltpu.VMEM((2, GROUP, 2, 2, *part), BF),
+            pltpu.VMEM(heads, BF),
             pltpu.VMEM(heads, BF),
             pltpu.VMEM(heads, BF),
             pltpu.VMEM(heads, BF),
@@ -515,26 +610,32 @@
             pltpu.VMEM((2, RING // 2, 2, 2, 2, 2, *part), BF),
             pltpu.VMEM((GROUP, 2, 2, *part), BF),
             pltpu.VMEM((GROUP, 2, 2, *part), BF),
-            pltpu.VMEM(heads, BF),
-            pltpu.VMEM(heads, BF),
-            pltpu.VMEM(heads, BF),
-            pltpu.VMEM(heads, BF),
-            pltpu.VMEM(wide, BF),
+            pltpu.VMEM(heads, F32),
+            pltpu.VMEM((GROUP, 8, ROWS), F32),
+            pltpu.VMEM((3, GROUP, 8, ROWS), F32),
+            pltpu.VMEM(heads, BF),
+            pltpu.VMEM(heads, BF),
+            pltpu.VMEM(heads, BF),
+            pltpu.VMEM(heads, BF),
             dma((3, 8)),
             dma((3, 8)),
-            dma((2, 2, RING // 2)),
-            dma((2, 2, RING // 2)),
+            dma((2, RING // 2, GROUP)),
+            dma((2, RING // 2, GROUP)),
             dma((2, RING // 2, 2)),
             dma((2, RING // 2, 2)),
-            dma,
-            dma,
+            dma((2, RING // 2, 2)),
+            dma((2, RING // 2, 2)),
+            dma((3, 2)),
+            dma((3, 2)),
+            dma((GROUP,)),
+            dma((GROUP,)),
         ],
         compiler_params=pltpu.CompilerParams(
             collective_id=0, has_side_effects=True, vmem_limit_bytes=56 * 1024 * 1024
         ),
         name="attention",
     )(
-        order, inverse, types_fwd, types_bwd, type_key[0],
+        order, types_fwd, types_bwd, type_key[0],
         query_fwd[0], key_fwd[0], value_fwd[0],
         query_bwd[0], key_bwd[0], value_bwd[0], grad_out[0], gate_fwd[0], norm_gain,
     )

time: 117 us -> 111 us (0.949)
  the two profiles are of different devices: /device:TPU:1 before, /device:TPU:11 now
where the time goes in v3:
time: 111 us
  Pallas kernels  106 us (95%)
  local copies, waits for them, and re-layouts  4.57 us (4%)
    pallas_call x1, Pallas kernels, body(): pl.pallas_call(kernel, out_shape=(jax.ShapeDtypeStruct(wide, BF), jax.Sha...  106 us
    unnamed x10, local copies, waits for them, and re-layouts  4.57 us

profile of v3, /device:TPU:11, one launch (start us, length us, event | category | flops | bytes accessed | tf_op | source)
XLA Modules:
  0.0 111.3 jit_solution(10059213281205690690)
XLA Ops:
  0.6 106.0 %attention.1 = (bf16[128,2048]{1,0:T(8,128)(2,1)}, bf16[128,2048]{1,0:T(8,128)(2,1)}, bf16[128,512]{1,0:T(8,128)(2,1)}, bf16[128,512]{1,0:T(8,128)(2,1)}) custom-call(s32[64]{0:T(128)} %bitcast.27, s32[1,128]{1,0:T(1,128)} %types_f.1, s32[1,128]{1,0:T(1,128)} %types_b.1, bf16[64,512]{1,0:T(8,128)(2,1)} %bitcast.26, bf16[128,2048]{1,0:T(8,128)(2,1)} %bitcast.16, ...), custom_call_target="tpu_custom_call" | custom-call | tf_op jit(solution)/shard_map/attention/pallas_call | solution.py:575
  106.7 0.0 copy-start
  106.7 1.9 %copy.21 = bf16[1,128,2048]{2,1,0:T(8,128)(2,1)} copy(bf16[1,128,2048]{2,1,0:T(8,128)(2,1)} %bitcast.15) | data formatting | bytes 1048576
  108.6 0.0 copy-done
  108.6 0.0 copy-start.2
  108.6 0.8 copy.22
  109.4 0.2 copy-done.2
  109.7 0.0 copy-start.1
  109.7 0.7 copy.23
  110.3 0.3 copy-done.1
  110.6 0.7 copy.24
Async XLA Ops:
  106.7 2.0 %copy-start = (bf16[128,2048]{1,0:T(8,128)(2,1)S(1)}, bf16[128,2048]{1,0:T(8,128)(2,1)}, u32[]{:S(2)}) copy-start(bf16[128,2048]{1,0:T(8,128)(2,1)} %get-tuple-element.9) | copy-start | bytes 1572868
  108.6 1.0 copy-start.2
  109.7 1.0 copy-start.1

commit v4 on v3

--- a/solution.py
+++ b/solution.py
@@ -73,8 +73,8 @@
     order, types_f, types_b, table, qf, kf, vf, qb, kb, vb, go, gate, gain,
     handed, query_grad, key_grad, value_grad,
     inverse, stage_q, stage_kv, in_qf, in_qb, in_go, in_gate, in_kvf, in_kvb,
-    ks, vs, kt, dk, dv, acc, acc_t, qs, gs, dgk, dgv, q_pick, g_pick,
-    dkv, sums, landed, total, dkv_in, att, norms, norms_in, dq, dq_in, gated, hand_in,
+    ks, vs, kt, dk, dv, acc, acc_t, qs, gs, qt, gt, dgk, dgv, q_wide, g_wide,
+    dkv, sums, landed, landed_half, total, dkv_in, att, norms, norms_in, dq, dq_in, gated, hand_in,
     a_send, a_recv, b_send, b_recv, g_send, g_recv, r_send, r_recv,
     n_send, n_recv, h_send, h_recv,
 ):
@@ -96,18 +96,18 @@
         + [ctx_of(z + 1, m), ctx_of(z - 1, m)]
         + [beside(d, s) for d in (1, -1) for s in range(GROUP)]
     )
-    started = []
+    sent = []
 
 
     def exchange(t, source, target, slot):
         copies = []
         for d, p in enumerate(peers):
             copy = remote(
-                source.at[p], target.at[slot], a_send.at[d, t], a_recv.at[d, t], ctx_of(z, p)
+                source.at[p], target.at[slot], a_send.at[t], a_recv.at[d, t], ctx_of(z, p)
             )
             copy.start()
             copies.append(copy)
-            started.append(copy)
+        sent.append((source.at[pl.ds(0, len(peers))], a_send.at[t]))
         return copies
 
     def stage_keys(t, types, keys, values):
@@ -144,11 +144,9 @@
         chunk = ((z - way * (step - 1) + RING) % RING) * GROUP
         view = target.at[pl.ds(chunk + first, count)]
         copy = remote(
-            view, view, send.at[lane, step - 1, part], recv.at[lane, step - 1, part],
-            ctx_of(z + way, m),
+            view, view, send.at[lane], recv.at[lane, step - 1, part], ctx_of(z + way, m)
         )
         copy.start()
-        started.append(copy)
         moving[t, lane, part] = copy
 
     def spread_b(step, d):
@@ -273,27 +271,32 @@
     for i in range(GROUP):
         for w in range(2):
             qs[w, i] = query_rows(in_qb, i, w)
-            g = query_rows(in_go, i, w).astype(F32) * shrink_rows(stretch[w][i])
+            g = query_rows(in_go, i, w).astype(F32) * (0.5 * shrink_rows(stretch[w][i]))
             gs[w, i] = g.astype(BF)
+            qt[w, :, span[i]] = qs[w, i].T
+            gt[w, :, span[i]] = gs[w, i].T
+            q_wide[w, i] = jnp.zeros((QROWS, 2 * HEAD), BF)
+            q_wide[w, i, :, columns(w)] = qs[w, i]
+            g_wide[w, i] = jnp.zeros((QROWS, 2 * HEAD), BF)
+            g_wide[w, i, :, columns(w)] = gs[w, i]
     key_over = lax.broadcasted_iota(jnp.int32, (BLOCK, QROWS), 0) - (
         lax.broadcasted_iota(jnp.int32, (BLOCK, QROWS), 1) % HALF
     )
 
     def slopes(k, v, q, g):
-        u = dot_nt(k, q) * (0.5 * SCALE)
-        grad = dot_nt(v, g)
+        u = (dot_nn(k, q) * (0.5 * SCALE)).astype(BF)
+        grad = dot_nn(v, g).astype(BF)
+        one = jnp.asarray(1.0, BF)
         t = jnp.tanh(u)
         ut = u * t
-        return u + ut, (0.5 + 0.5 * t) * (1.0 + (u - ut)) * grad
+        return u + ut, (one + t) * (one + (u - ut)) * grad
 
     def seen(over, bound, value):
-        return jnp.where(over <= bound, value, 0.0).astype(BF)
+        return jnp.where(over <= bound, value, jnp.zeros_like(value)).astype(BF)
 
     def backward_full(b, _):
         q, g = qs[1].reshape(GROUP * QROWS, HEAD), gs[1].reshape(GROUP * QROWS, HEAD)
-        p, s = slopes(ks[b], vs[b], q, g)
-        p = p.astype(BF)
-        s = s.astype(BF)
+        p, s = slopes(ks[b], vs[b], qt[1], gt[1])
         dv[stretches(b)] = dot_nn(p, g).reshape(-1, HALF, HEAD)
         dk[stretches(b)] = dot_nn(s, q).reshape(-1, HALF, HEAD)
         acc_t[1] += dot_nn(kt[b], s)
@@ -301,34 +304,29 @@
 
     def backward_edge(i):
         at = last - quart[i]
-        q, g = qs[1, i], gs[1, i]
-        p, s = slopes(ks[at], vs[at], q, g)
+        p, s = slopes(ks[at], vs[at], qt[1, :, span[i]], gt[1, :, span[i]])
         p = seen(key_over, bound_high(i), p)
         s = seen(key_over, bound_high(i), s)
-        dgv[i] = dot_nn(p, g)
-        dgk[i] = dot_nn(s, q)
+        dgv[i] = dot_nn(p, gs[1, i])
+        dgk[i] = dot_nn(s, qs[1, i])
         acc_t[1, :, span[i]] += dot_nn(kt[at], s)
 
     def backward_choice(n, _):
-        zero = jnp.zeros((QROWS, HEAD), BF)
-        ps, ss = [], []
+        ps, ss, qw, gw = [], [], [], []
         for i in range(GROUP):
             is_low, at, w = choice(i, n)
-            q, g = qs[w, i], gs[w, i]
-            p, s = slopes(ks[at], vs[at], q, g)
+            p, s = slopes(ks[at], vs[at], qt[w, :, span[i]], gt[w, :, span[i]])
             p = seen(key_over, bound_low(i, n), p)
             s = seen(key_over, bound_low(i, n), s)
             part = dot_nn(kt[at], s)
             acc_t[0, :, span[i]] += jnp.where(is_low, part, 0.0)
             acc_t[1, :, span[i]] += jnp.where(is_low, 0.0, part)
-            g_pick[span[i], :HEAD] = jnp.where(is_low, g, zero)
-            g_pick[span[i], HEAD:] = jnp.where(is_low, zero, g)
-            q_pick[span[i], :HEAD] = jnp.where(is_low, q, zero)
-            q_pick[span[i], HEAD:] = jnp.where(is_low, zero, q)
             ps.append(p)
             ss.append(s)
-        both_v = dot_nn(jnp.concatenate(ps, 1), g_pick[...])
-        both_k = dot_nn(jnp.concatenate(ss, 1), q_pick[...])
+            qw.append(q_wide[w, i])
+            gw.append(g_wide[w, i])
+        both_v = dot_nn(jnp.concatenate(ps, 1), jnp.concatenate(gw, 0))
+        both_k = dot_nn(jnp.concatenate(ss, 1), jnp.concatenate(qw, 0))
         dv[stretches(n)] += both_v[:, :HEAD].reshape(-1, HALF, HEAD)
         dk[stretches(n)] += both_k[:, :HEAD].reshape(-1, HALF, HEAD)
         high_v, high_k = both_v[:, HEAD:], both_k[:, HEAD:]
@@ -365,45 +363,44 @@
             for half in range(2):
                 p = order[2 * (chunk + c) + half]
                 dkv[chunk + c, 0, half] = (dk[p] * SCALE).astype(BF)
-                dkv[chunk + c, 1, half] = dv[p].astype(BF)
+                dkv[chunk + c, 1, half] = (dv[p] * 2.0).astype(BF)
             return 0
 
         lax.fori_loop(0, GROUP, store, 0)
 
     reducing = {}
 
-    def reduce(step, lane, part):
-        way = (1, -1)[lane]
-        chunk = ((z + way * (RING // 2 - step) + RING) % RING) * GROUP
-        mine = pl.ds(chunk + chips[part], 2)
-        if step == 0 or (step == 1 and part != lane):
-            source = dkv.at[mine]
-        else:
-            reducing[lane, part].wait_recv()
-            arrived = landed[lane, step - 1, part].astype(F32)
-            sums[lane, step - 1, part] = (dkv[mine].astype(F32) + arrived).astype(BF)
-            source = sums.at[lane, step - 1, part]
-        copy = remote(
-            source, landed.at[lane, step, part],
-            r_send.at[lane, step, part], r_recv.at[lane, step, part], ctx_of(z + way, m),
-        )
-        copy.start()
-        started.append(copy)
-        reducing[lane, part] = copy
-
-    def reduce_fresh(step):
-        for lane in range(2):
-            reduce(step, lane, 1 - lane)
-
-    def reduce_chained(step):
-        for lane in range(2):
-            reduce(step, lane, lane)
+    def reduce(step, part):
+        for lane, way in enumerate((1, -1)):
+            chunk = ((z + way * (RING // 2 - step) + RING) % RING) * GROUP
+            mine = pl.ds(chunk + chips[part], 2)
+            if step > 0:
+                reducing[lane, part].wait_recv()
+                terms = dkv[mine].astype(F32)
+                partial = sums.at[lane, step - 1, part]
+            if step == 0:
+                source, target = dkv.at[mine, :, lane], landed_half.at[lane, part]
+            else:
+                if step == 1:
+                    arrived = landed_half[lane, part].astype(F32)
+                    partial[:, :, lane] = (terms[:, :, lane] + arrived).astype(BF)
+                    partial[:, :, 1 - lane] = dkv[mine, :, 1 - lane]
+                else:
+                    arrived = landed[lane, step - 2, part].astype(F32)
+                    partial[...] = (terms + arrived).astype(BF)
+                source, target = partial, landed.at[lane, step - 1, part]
+            copy = remote(
+                source, target, r_send.at[lane], r_recv.at[lane, step, part],
+                ctx_of(z + way, m),
+            )
+            copy.start()
+            reducing[lane, part] = copy
 
     store_chunk(RING // 2)
-    reduce_chained(0)
+    reduce(0, 1)
+    reduce(0, 0)
     for distance in (3, -3):
         store_chunk(distance)
-    reduce_fresh(1)
     for i in range(GROUP):
         put_rows(
             dq, i, (acc_t[0, :, span[i]] * SCALE).T, (acc_t[1, :, span[i]] * SCALE).T
@@ -475,10 +472,9 @@
         for d, p in enumerate(peers):
             copy = remote(
                 norms.at[pairs], norms_in.at[d, pairs],
-                n_send.at[d, part], n_recv.at[d, part], ctx_of(z, p),
+                n_send, n_recv.at[d, part], ctx_of(z, p),
             )
             copy.start()
-            started.append(copy)
             norm_copies[part].append(copy)
 
     def hand_rows(part):
@@ -495,36 +491,34 @@
                     * in_gate[i, :, g].astype(F32)
                 ).astype(BF)
             copy = remote(
-                gated.at[i], hand_in.at[m], h_send.at[i], h_recv.at[m], beside(1, i)
+                gated.at[i], hand_in.at[m], h_send, h_recv.at[m], beside(1, i)
             )
             copy.start()
-            started.append(copy)
 
     acc[...] = jnp.zeros_like(acc)
     forward_full(0)
-    reduce_chained(1)
+    reduce(1, 1)
+    reduce(1, 0)
     forward_edge(0)
-    forward_choice(0, 0, middle)
-    reduce_fresh(2)
-    forward_choice(0, middle, half_blocks)
+    forward_choice(0, 0, half_blocks)
     measure_rows(0)
-    reduce_chained(2)
+    reduce(2, 1)
     forward_full(1)
-    reduce_fresh(3)
+    reduce(2, 0)
     arrive(gate_copies)
     hand_rows(0)
     forward_edge(1)
-    forward_choice(1, 0, middle)
-    reduce_chained(3)
-    forward_choice(1, middle, half_blocks)
+    forward_choice(1, 0, half_blocks)
     measure_rows(1)
+    reduce(3, 1)
+    hand_rows(1)
+    reduce(3, 0)
     arrive(dq_copies)
     for h in range(GROUP):
         for g in range(4):
             for half in range(2):
                 rows = slice(half * HALF, (half + 1) * HALF)
                 query_grad[rows, columns(h * 4 + g)] = dq_in[h, half, g]
-    hand_rows(1)
 
 
     for part in (1, 0):
@@ -532,16 +526,15 @@
             reducing[lane, part].wait_recv()
         total[pl.ds(chips[part], 2)] = (
             dkv[pl.ds(z * GROUP + chips[part], 2)].astype(F32)
-            + landed[0, RING // 2 - 1, part].astype(F32)
-            + landed[1, RING // 2 - 1, part].astype(F32)
+            + landed[0, RING // 2 - 2, part].astype(F32)
+            + landed[1, RING // 2 - 2, part].astype(F32)
         ).astype(BF)
         for d in ((1, 2), (0,))[1 - part]:
             copy = remote(
-                total.at[peers[d]], dkv_in.at[m], a_send.at[d, 7], a_recv.at[d, 7],
+                total.at[peers[d]], dkv_in.at[m], a_send.at[7], a_recv.at[d, 7],
                 ctx_of(z, peers[d]),
             )
             copy.start()
-            started.append(copy)
             moving[2, 0, d] = copy
     dkv_in[m] = total[m]
     gathered(2)
@@ -551,13 +544,26 @@
             key_grad[rows, columns(h)] = dkv_in[h, 0, half]
             value_grad[rows, columns(h)] = dkv_in[h, 1, half]
     for h in range(GROUP):
-        remote(gated.at[h], hand_in.at[h], h_send.at[h], h_recv.at[h], beside(1, h)).wait_recv()
+        remote(gated.at[h], hand_in.at[h], h_send, h_recv.at[h], beside(1, h)).wait_recv()
         for g in range(4):
             for half in range(2):
                 rows = slice(half * HALF, (half + 1) * HALF)
                 handed[rows, columns(h * 4 + g)] = hand_in[h, half, g]
-    for copy in started:
-        copy.wait_send()
+    ring = pl.ds(0, GROUP * RING // 2 - 2)
+    for lane in range(2):
+        sent.append((in_kvb.at[ring], b_send.at[lane]))
+        sent.append((in_kvf.at[ring], g_send.at[lane]))
+        sent.append((dkv.at[ring], r_send.at[lane]))
+    sent.append((total.at[pl.ds(0, len(peers))], a_send.at[7]))
+    sent.append((norms_in, n_send))
+    sent.append((gated, h_send))
+    for view, send in sent:
+        remote(view, view, send, h_recv.at[0], ctx_of(z, peers[0])).wait_send()
+
+
+def copy_kernel(*refs):
+    for source, target in zip(refs[:4], refs[4:], strict=True):
+        target[...] = source[...]
 
 
 def body(
@@ -601,13 +607,16 @@
             pltpu.VMEM((2, HEAD, GROUP * QROWS), F32),
             pltpu.VMEM((2, GROUP, QROWS, HEAD), BF),
             pltpu.VMEM((2, GROUP, QROWS, HEAD), BF),
+            pltpu.VMEM((2, HEAD, GROUP * QROWS), BF),
+            pltpu.VMEM((2, HEAD, GROUP * QROWS), BF),
             pltpu.VMEM((GROUP, BLOCK, HEAD), F32),
             pltpu.VMEM((GROUP, BLOCK, HEAD), F32),
-            pltpu.VMEM((GROUP * QROWS, 2 * HEAD), BF),
-            pltpu.VMEM((GROUP * QROWS, 2 * HEAD), BF),
+            pltpu.VMEM((2, GROUP, QROWS, 2 * HEAD), BF),
+            pltpu.VMEM((2, GROUP, QROWS, 2 * HEAD), BF),
             pltpu.VMEM(pairs, BF),
             pltpu.VMEM((2, RING // 2 - 1, 2, 2, 2, 2, *part), BF),
-            pltpu.VMEM((2, RING // 2, 2, 2, 2, 2, *part), BF),
+            pltpu.VMEM((2, RING // 2 - 1, 2, 2, 2, 2, *part), BF),
+            pltpu.VMEM((2, 2, 2, 2, *part), BF),
             pltpu.VMEM((GROUP, 2, 2, *part), BF),
             pltpu.VMEM((GROUP, 2, 2, *part), BF),
             pltpu.VMEM(heads, F32),
@@ -617,17 +626,17 @@
             pltpu.VMEM(heads, BF),
             pltpu.VMEM(heads, BF),
             pltpu.VMEM(heads, BF),
+            dma((8,)),
             dma((3, 8)),
-            dma((3, 8)),
+            dma((2,)),
             dma((2, RING // 2, GROUP)),
-            dma((2, RING // 2, GROUP)),
+            dma((2,)),
             dma((2, RING // 2, 2)),
+            dma((2,)),
             dma((2, RING // 2, 2)),
-            dma((2, RING // 2, 2)),
-            dma((2, RING // 2, 2)),
+            dma,
             dma((3, 2)),
-            dma((3, 2)),
-            dma((GROUP,)),
+            dma,
             dma((GROUP,)),
         ],
         compiler_params=pltpu.CompilerParams(
@@ -639,7 +648,15 @@
         query_fwd[0], key_fwd[0], value_fwd[0],
         query_bwd[0], key_bwd[0], value_bwd[0], grad_out[0], gate_fwd[0], norm_gain,
     )
-    return handed[None], query_grad[None], key_grad[None], value_grad[None]
+    outs = (handed, query_grad, key_grad, value_grad)
+    outs = pl.pallas_call(
+        copy_kernel,
+        out_shape=tuple(jax.ShapeDtypeStruct(o.shape, o.dtype) for o in outs),
+        in_specs=[VMEM] * 4,
+        out_specs=(VMEM,) * 4,
+        name="finish",
+    )(*outs)
+    return tuple(o[None] for o in outs)
 
 
 def solution(mesh):

time: 111 us -> 104 us (0.937)
  local copies, waits for them, and re-layouts: 4.57 us -> 0 us
  Pallas kernels: 106 us -> 103 us
    pallas_call x1, Pallas kernels: 106 us -> 101 us  [body(): pl.pallas_call(kernel, out_shape=(jax.ShapeDtypeStruct(wide, BF), jax.Sha...]
    unnamed x10 -> x0, local copies, waits for them, and re-layouts: 4.57 us -> none
    pallas_call x0 -> x1, Pallas kernels: none -> 2.34 us  [body(): pl.pallas_call(copy_kernel, out_shape=tuple((jax.ShapeDtypeStruct(o.shape...]
where the time goes in v4:
time: 104 us
  Pallas kernels  103 us (99%)
    pallas_call x1, Pallas kernels, body(): pl.pallas_call(kernel, out_shape=(jax.ShapeDtypeStruct(wide, BF), jax.Sha...  101 us
    pallas_call x1, Pallas kernels, body(): pl.pallas_call(copy_kernel, out_shape=tuple((jax.ShapeDtypeStruct(o.shape...  2.34 us

profile of v4, /device:TPU:11, one launch (start us, length us, event | category | flops | bytes accessed | tf_op | source)
XLA Modules:
  0.0 104.0 jit_solution(4075910170849003441)
XLA Ops:
  0.6 101.0 %attention.1 = (bf16[128,2048]{1,0:T(8,128)(2,1)}, bf16[128,2048]{1,0:T(8,128)(2,1)}, bf16[128,512]{1,0:T(8,128)(2,1)}, bf16[128,512]{1,0:T(8,128)(2,1)}) custom-call(s32[64]{0:T(128)} %bitcast.23, s32[1,128]{1,0:T(1,128)} %types_f.1, s32[1,128]{1,0:T(1,128)} %types_b.1, bf16[64,512]{1,0:T(8,128)(2,1)} %bitcast.22, bf16[128,2048]{1,0:T(8,128)(2,1)} %bitcast.14, ...), custom_call_target="tpu_custom_call" | custom-call | tf_op jit(solution)/shard_map/attention/pallas_call | solution.py:581
  101.7 2.3 %finish.1 = (bf16[128,2048]{1,0:T(8,128)(2,1)}, bf16[128,2048]{1,0:T(8,128)(2,1)}, bf16[128,512]{1,0:T(8,128)(2,1)}, bf16[128,512]{1,0:T(8,128)(2,1)}) custom-call(bf16[128,2048]{1,0:T(8,128)(2,1)} %get-tuple-element.12.refs_0_, bf16[128,2048]{1,0:T(8,128)(2,1)} %get-tuple-element.13.refs_1_, bf16[128,512]{1,0:T(8,128)(2,1)} %get-tuple-element.14.refs_2_, ...), custom_call_target="tpu_custom_call" | custom-call | tf_op jit(solution)/shard_map/finish/pallas_call | solution.py:652

commit v5 on v4

--- a/solution.py
+++ b/solution.py
@@ -70,14 +70,20 @@
 
 
 def kernel(
-    order, types_f, types_b, table, qf, kf, vf, qb, kb, vb, go, gate, gain,
+    order, types_f, types_b, table, kb, vb, gain, qb_far, go_far, kf_far, vf_far, qf_far, gate_far,
     handed, query_grad, key_grad, value_grad,
     inverse, stage_q, stage_kv, in_qf, in_qb, in_go, in_gate, in_kvf, in_kvb,
     ks, vs, kt, dk, dv, acc, acc_t, qs, gs, qt, gt, dgk, dgv, q_wide, g_wide,
     dkv, sums, landed, landed_half, total, dkv_in, att, norms, norms_in, dq, dq_in, gated, hand_in,
     a_send, a_recv, b_send, b_recv, g_send, g_recv, r_send, r_recv,
     n_send, n_recv, h_send, h_recv,
+    qb, go, kf, vf, qf, gate, l_sem,
 ):
+    loads = {}
+    near = ((qb_far, qb), (go_far, go), (kf_far, kf), (vf_far, vf), (qf_far, qf), (gate_far, gate))
+    for n, (far, here) in enumerate(near):
+        loads[n] = pltpu.make_async_copy(far, here, l_sem.at[n])
+        loads[n].start()
     z, m, peers = place()
     x = m // 2
     members = (m, *peers)
@@ -180,26 +186,32 @@
     kvb_copies = exchange(0, stage_kv.at[1], in_kvb, z * GROUP + m)
     in_kvb[z * GROUP + m] = stage_kv[1, m]
     spread_b(1, 0)
+    loads[0].wait()
     stage_rows(1, qb)
     qb_copies = exchange(1, stage_q.at[1], in_qb, m)
     kvb_copies[0].wait_recv()
     spread_b(1, 1)
     in_qb[m] = stage_q[1, m]
+    loads[1].wait()
     stage_rows(2, go)
     go_copies = exchange(2, stage_q.at[2], in_go, m)
     in_go[m] = stage_q[2, m]
     for d in (1, 2):
         kvb_copies[d].wait_recv()
         spread_b(1, d + 1)
+    loads[2].wait()
+    loads[3].wait()
     stage_keys(0, types_f, kf, vf)
     spread_b(2, 0)
     kvf_copies = exchange(3, stage_kv.at[0], in_kvf, z * GROUP + m)
     in_kvf[z * GROUP + m] = stage_kv[0, m]
     spread_b(2, 1)
+    loads[4].wait()
     stage_rows(0, qf)
     qf_copies = exchange(4, stage_q.at[0], in_qf, m)
     in_qf[m] = stage_q[0, m]
     spread_b(2, 2)
+    loads[5].wait()
     stage_rows(3, gate)
     gate_copies = exchange(6, stage_q.at[3], in_gate, m)
     in_gate[m] = stage_q[3, m]
@@ -342,18 +354,18 @@
     middle = half_blocks // 2
     acc_t[...] = jnp.zeros_like(acc_t)
     spread_f(2, 0)
-    lax.fori_loop(0, 3, backward_full, 0)
+    lax.fori_loop(0, 5, backward_full, 0)
     spread_f(2, 1)
-    lax.fori_loop(3, 6, backward_full, 0)
+    lax.fori_loop(5, half_blocks, backward_full, 0)
     spread_f(3, 0)
-    lax.fori_loop(6, half_blocks, backward_full, 0)
     for i in range(GROUP):
         backward_edge(i)
+    lax.fori_loop(0, 2, backward_choice, 0)
     spread_f(3, 1)
-    lax.fori_loop(0, 2, backward_choice, 0)
+    lax.fori_loop(2, 5, backward_choice, 0)
     for part in range(2):
         spread_f(4, part)
-    lax.fori_loop(2, half_blocks, backward_choice, 0)
+    lax.fori_loop(5, half_blocks, backward_choice, 0)
 
 
     def store_chunk(distance):
@@ -586,7 +598,7 @@
             jax.ShapeDtypeStruct(narrow, BF),
             jax.ShapeDtypeStruct(narrow, BF),
         ),
-        in_specs=[smem] + [VMEM] * 12,
+        in_specs=[smem] + [VMEM] * 6 + [pl.BlockSpec(memory_space=pl.ANY)] * 6,
         out_specs=(VMEM,) * 4,
         scratch_shapes=[
             pltpu.SMEM((2 * CTX,), jnp.int32),
@@ -638,15 +650,21 @@
             dma((3, 2)),
             dma,
             dma((GROUP,)),
+            pltpu.VMEM(wide, BF),
+            pltpu.VMEM(wide, BF),
+            pltpu.VMEM(narrow, BF),
+            pltpu.VMEM(narrow, BF),
+            pltpu.VMEM(wide, BF),
+            pltpu.VMEM(wide, BF),
+            dma((6,)),
         ],
         compiler_params=pltpu.CompilerParams(
             collective_id=0, has_side_effects=True, vmem_limit_bytes=56 * 1024 * 1024
         ),
         name="attention",
     )(
-        order, types_fwd, types_bwd, type_key[0],
-        query_fwd[0], key_fwd[0], value_fwd[0],
-        query_bwd[0], key_bwd[0], value_bwd[0], grad_out[0], gate_fwd[0], norm_gain,
+        order, types_fwd, types_bwd, type_key[0], key_bwd[0], value_bwd[0], norm_gain,
+        query_bwd[0], grad_out[0], key_fwd[0], value_fwd[0], query_fwd[0], gate_fwd[0],
     )
     outs = (handed, query_grad, key_grad, value_grad)
     outs = pl.pallas_call(

time: 104 us -> 102 us (0.981)
  Pallas kernels: 103 us -> 101 us
    pallas_call x1, Pallas kernels: 101 us -> 98.5 us  [body(): pl.pallas_call(kernel, out_shape=(jax.ShapeDtypeStruct(wide, BF), jax.Sha...]
where the time goes in v5:
time: 102 us; the launch traced here: 101 us
  Pallas kernels  101 us (99%)
    pallas_call x1, Pallas kernels, body(): pl.pallas_call(kernel, out_shape=(jax.ShapeDtypeStruct(wide, BF), jax.Sha...  98.5 us
    pallas_call x1, Pallas kernels, body(): pl.pallas_call(copy_kernel, out_shape=tuple((jax.ShapeDtypeStruct(o.shape...  2.34 us

profile of v5, /device:TPU:11, one launch (start us, length us, event | category | flops | bytes accessed | tf_op | source)
XLA Modules:
  0.0 101.5 jit_solution(10445676537293048714)
XLA Ops:
  0.6 98.5 %attention.1 = (bf16[128,2048]{1,0:T(8,128)(2,1)}, bf16[128,2048]{1,0:T(8,128)(2,1)}, bf16[128,512]{1,0:T(8,128)(2,1)}, bf16[128,512]{1,0:T(8,128)(2,1)}) custom-call(s32[64]{0:T(128)} %bitcast.23, s32[1,128]{1,0:T(1,128)} %types_f.1, s32[1,128]{1,0:T(1,128)} %types_b.1, bf16[64,512]{1,0:T(8,128)(2,1)} %bitcast.22, bf16[128,512]{1,0:T(8,128)(2,1)} %bitcast.18, ...), custom_call_target="tpu_custom_call" | custom-call | tf_op jit(solution)/shard_map/attention/pallas_call | solution.py:593
  99.2 2.3 %finish.1 = (bf16[128,2048]{1,0:T(8,128)(2,1)}, bf16[128,2048]{1,0:T(8,128)(2,1)}, bf16[128,512]{1,0:T(8,128)(2,1)}, bf16[128,512]{1,0:T(8,128)(2,1)}) custom-call(bf16[128,2048]{1,0:T(8,128)(2,1)} %get-tuple-element.12.refs_0_, bf16[128,2048]{1,0:T(8,128)(2,1)} %get-tuple-element.13.refs_1_, bf16[128,512]{1,0:T(8,128)(2,1)} %get-tuple-element.14.refs_2_, ...), custom_call_target="tpu_custom_call" | custom-call | tf_op jit(solution)/shard_map/finish/pallas_call | solution.py:670
